TPU v7x, 32 devices: a whole 2x2x4 slice. The times are simulated.
32 devices in a mesh: row: 4 (over x, core), col: 8 (over z, y).
Axes of the slice: x: 2, y: 2, z: 4, core: 2. Of those that a mesh axis runs over, the one named last changes fastest.
Arguments:
- measured: float32 [16, 64, 1024], P(None, 'row', 'col')
- regions: int32 [4, 64], P('row', 'col'), may hold values from 0 to 63
- kernels: float32 [64, 9, 9], replicated, may hold values from 0 to 0.024691358
- radius: int32 [64], replicated, may hold values from 1 to 4, as said below
Outputs:
- solution: float32 [16, 64, 1024], P(None, 'row', 'col')
- residual: float32 [16, 64, 1024], P(None, 'row', 'col')
Inputs may be any that keep to these rules, and one draw needn't show every extreme that they name: Some kernel has radius 4.
All inputs are finite; a program needn't handle non-finite values.
Results may differ from a plain program's by a relative error of at most 0.0029.
Values sent between devices are 32-bit elements; how exact they have to be, the bound alone decides.
No kernel may reach another device: no remote copies, remote signals or barrier semaphores. Data moves between devices by JAX's collectives and lax.ppermute only.
A program may use at most 64 MiB of HBM per device.

v0:
```python
import functools

import jax
import jax.numpy as jnp
from jax import lax
from jax.experimental import pallas as pl
from jax.experimental.pallas import tpu as pltpu
from jax.sharding import PartitionSpec as P

R = 4
K = 9
SUB = 16
REG = 64
DAMPING = 0.1

LANES = 128
HALO = 32
PACK = LANES // HALO
NB = 4

F32 = jnp.float32
BF16 = jnp.bfloat16
NN = (((1,), (0,)), ((), ()))
NT = (((1,), (1,)), ((), ()))
HIGHEST = lax.Precision.HIGHEST
VMEM = pl.BlockSpec(memory_space=pltpu.VMEM)
SMEM = pl.BlockSpec(memory_space=pltpu.SMEM)
def params(mib):
    return pltpu.CompilerParams(vmem_limit_bytes=mib << 20)


def split(value):
    high = value.astype(BF16)
    return high, (value - high.astype(F32)).astype(BF16)


def lane_iota(rows):
    return lax.broadcasted_iota(jnp.int32, (rows, LANES), 1)


def row_of(ref, index, row):
    frames, rows = ref.shape[1], ref.shape[2]
    flat = ref.reshape(ref.shape[0] * frames * rows, LANES)
    return flat[pl.ds(index * frames * rows + row, frames, stride=rows), :]


def place():
    r, c = lax.axis_index("row"), lax.axis_index("col")
    q = (r ^ c) & 1
    beside = jnp.where(q == 0, c > 0, c < lax.axis_size("col") - 1)
    return r, q, beside.astype(jnp.int32)


def pack_tile(tile, index, out, slot):
    q = place()[1]
    for group in range(SUB // PACK):
        packed = None
        for m in range(PACK):
            line = row_of(tile, index, group * PACK + m)
            line = pltpu.roll(line, HALO * m + HALO * q, 1)
            lanes = lane_iota(line.shape[0])
            packed = line if packed is None else jnp.where(lanes >= HALO * m, line, packed)
        out[slot + group] = packed


def first_kernel(tile, radius_ref, out, reach_ref):
    for index in range(tile.shape[0]):
        pack_tile(tile, index, out, index * (SUB // PACK))
    reach_ref[...] = jnp.zeros_like(reach_ref)
    reach_ref[0:1, :REG] = radius_ref[...]


def pack_kernel(nlabels, packed, *refs):
    labels, tiles, (out, tags) = refs[:nlabels], refs[nlabels:-2], refs[-2:]
    slot = packed.shape[0]
    out[:slot] = packed[...]
    for tile in tiles:
        pack_tile(tile, 0, out, slot)
        slot += SUB // PACK
    tags[...] = jnp.zeros((16, LANES), F32)
    line = 0
    for ref in labels:
        height, width = ref.shape
        tags[line : line + height, :width] = (ref[...] + 1).astype(F32)
        line += height
    out[slot] = tags[...]


def stage_weights(bt, s, transposed):
    zero = jnp.zeros((LANES, LANES), BF16)

    def block(a):
        return bt[s, a] if 0 <= a < K else zero

    blocks = []
    for t in range(5):
        if transposed:
            index = [[2 * t + i - o for o in range(2)] for i in range(2)]
        else:
            index = [[8 - 2 * t + o - i for i in range(2)] for o in range(2)]
        blocks.append(
            jnp.concatenate([jnp.concatenate([block(a) for a in line], 1) for line in index], 0)
        )
    return blocks


class Rows:
    def __init__(self, rows, xor):
        self.rows, self.xor = rows, xor
        self.r, self.q, self.beside = place()
        self.down = (self.r >> 1) if xor else 0
        lanes = lane_iota(16)
        start = (LANES - HALO) * self.q
        self.in_halo = (lanes >= start) & (lanes < start + HALO)

    def block(self, k):
        return (k & 2) + ((k ^ self.r ^ self.down) & 1) if self.xor else k

    def turn(self, i, last):
        return i + self.down * (last - 2 * i) if self.xor else i

    def each(self, body, count, first=0):
        if self.xor:
            for s in range(first, count):
                body(s)
        else:
            lax.fori_loop(0, self.rows, lambda s, c: (body(s), c)[1], 0)

    def inside(self):
        mask = jnp.where(self.in_halo, self.beside.astype(F32), 1.0)
        return jnp.concatenate([mask, mask], 1)

    def own(self):
        return (self.block(0), self.block(1)) if self.xor else (self.r, self.r ^ 1)


def tables(taps_ref, radius_ref):
    radius = radius_ref[0:1, :REG]
    high, low, total = [], [], jnp.zeros((1, REG), F32)
    b = lax.broadcasted_iota(jnp.int32, (K, REG), 0)
    for a in range(K):
        reach = jnp.maximum(jnp.abs(b - R), abs(a - R))
        taps = jnp.where(reach <= radius, 0.5 * taps_ref[a], 0.0)
        total = total + jnp.sum(taps, axis=0, keepdims=True)
        for part, value in zip((high, low), split(taps)):
            part.append(value)
    squares = total * total
    mean = jnp.sum(squares, axis=1, keepdims=True) * (1.0 / REG)
    return high, low, 0.5 * jnp.sqrt(mean * jnp.max(squares, axis=1, keepdims=True))


def make_bands(where, blocks, high, low, labels, halo, base_ref, bth, btl):
    lanes = lane_iota(8)
    count = len(blocks)
    hots = []
    for j in range(count):
        own = jnp.broadcast_to(labels[j], (8, LANES))
        beside = jnp.broadcast_to(halo[count * (SUB // PACK) + j // 16, j % 16 : j % 16 + 1, :], (8, LANES))
        left = jnp.where(lanes < 2, pltpu.roll(beside, LANES - 6, 1), pltpu.roll(own, 2, 1))
        right = jnp.where(lanes < 6, pltpu.roll(own, LANES - 2, 1), pltpu.roll(beside, 6, 1))
        window = jnp.where(where.q == 0, left, right)
        diagonal = lanes == lax.broadcasted_iota(jnp.int32, (8, LANES), 0)
        column = jnp.sum(jnp.where(diagonal, window, 0.0), axis=1, keepdims=True)
        hots.append((column == (lanes[:, :REG] + 1).astype(F32)).astype(F32))
    hot = jnp.concatenate(hots, 0).astype(BF16)
    b = lax.broadcasted_iota(jnp.int32, (K, LANES), 0)
    spread = (lax.broadcasted_iota(jnp.int32, (K, LANES), 1) == (LANES + R - b) % LANES).astype(BF16)
    for a in range(K):
        base = None
        for part in (high, low):
            picked = lax.dot_general(hot, part[a], NT, preferred_element_type=F32).astype(BF16)
            line = lax.dot_general(picked, spread, NN, preferred_element_type=F32)
            base = line if base is None else base + line
        for j in range(count):
            base_ref[j, a] = base[8 * j : 8 * j + 8]
    for j, s in enumerate(blocks):
        for a in range(K):
            squares = base_ref[j, where.turn(a, K - 1)]
            for c in range(LANES // SUB):
                band = jnp.broadcast_to(squares[c : c + 1], (SUB, LANES))
                band = pltpu.roll(band, SUB * c, 1, stride=1, stride_axis=0)
                for ref, value in zip((bth, btl), split(band)):
                    ref[s, a, c * SUB : (c + 1) * SUB, :] = value


def make_window(where, blocks, tiles, halo, uh, ul):
    for j, (s, (ref, index)) in enumerate(zip(blocks, tiles)):
        for p in range(SUB // 2):
            parts = []
            for i in (where.turn(2 * p, SUB - 1), where.turn(2 * p + 1, SUB - 1)):
                line = pltpu.roll(row_of(ref, index, i), HALO + (LANES - 2 * HALO) * where.q, 1)
                edge = halo[j * (SUB // PACK) + i // PACK]
                edge = pltpu.roll(edge, (LANES - HALO * (i % PACK) + (LANES - HALO) * where.q) % LANES, 1)
                parts.append(jnp.where(where.in_halo, edge, line))
            for out, value in zip((uh, ul), split(jnp.concatenate(parts, 1))):
                out[s * (SUB // 2) + p] = value


def product(high, low, wh, wl, dims):
    both = lax.dot_general(jnp.concatenate([high, low], 0), wh, dims, preferred_element_type=F32)
    third = lax.dot_general(high, wl, dims, preferred_element_type=F32)
    return both[: high.shape[0]] + both[high.shape[0] :] + third


def spread_rows(bands, uh, ul, base, acc, s):
    wh, wl = (stage_weights(*bands(s, i), True) for i in range(2))
    start = (s - base) * 8
    high = uh[pl.ds(start, 8)].reshape(128, 2 * LANES)
    low = ul[pl.ds(start, 8)].reshape(128, 2 * LANES)
    for t in range(5):
        out = product(high, low, wh[t], wl[t], NN).reshape(8, 16, 2 * LANES)
        acc[pl.ds(s * 8 + 4 - t, 8)] += out


def gather_rows(bands, vh, vl, s):
    wh, wl = (stage_weights(*bands(s, i), False) for i in range(2))
    total = None
    for t in range(5):
        high = vh[pl.ds(s * 8 + t, 8)].reshape(128, 2 * LANES)
        low = vl[pl.ds(s * 8 + t, 8)].reshape(128, 2 * LANES)
        out = product(high, low, wh[t], wl[t], NT)
        total = out if total is None else total + out
    return total.reshape(8, 16, 2 * LANES)


def halves(value):
    return jnp.where(
        lane_iota(16) < LANES // 2,
        pltpu.roll(value[:, :LANES], LANES - HALO, 1),
        pltpu.roll(value[:, LANES:], HALO, 1),
    )


def slots_of(tiles):
    return [(ref, index) for ref in tiles for index in range(ref.shape[0])]


def near_kernel(rows, xor, ntiles, taps_ref, radius_ref, labels, halo, *refs):
    tiles = slots_of(refs[:ntiles])
    bth, btl, acc, acc1, real_ref, base_ref, uh, ul, vh, vl = refs[ntiles:]
    where = Rows(rows, xor)
    blocks = [where.block(k) for k in range(len(tiles))]
    high, low, shift = tables(taps_ref, radius_ref)
    real_ref[...] = jnp.broadcast_to(shift, real_ref.shape)
    lines = [labels[j : j + 1, :] for j in range(len(tiles))]
    make_bands(where, blocks, high, low, lines, halo, base_ref, bth, btl)
    make_window(where, blocks, tiles, halo, uh, ul)
    acc[...] = jnp.zeros_like(acc)
    bands = lambda s, i: ((bth, btl)[i], s)
    where.each(lambda s: spread_rows(bands, uh, ul, 0, acc, s), len(tiles))
    if xor:
        blank = jnp.zeros((2, 16, 2 * LANES), BF16)
        for ref in (vh, vl):
            ref[0:2] = blank
        for ref, value in zip((vh, vl), split(acc[2:12] * where.inside()[None])):
            ref[2:12] = value
        for ref, value in zip((uh, ul), split(gather_rows(bands, vh, vl, 0))):
            ref[0:8] = value
        acc1[...] = jnp.zeros_like(acc1)
        spread_rows(bands, uh, ul, 0, acc1, 0)


def main_kernel(rows, xor, ndev, ntiles, taps_ref, radius_ref, real_ref, nbh, nbl, nacc, nacc1, *refs):
    if ntiles:
        labels, halo = refs[:2]
        tiles = slots_of(refs[2 : 2 + ntiles])
        refs = refs[2 + ntiles :]
    gram_ref, keep_ref, send_ref, uh, ul, fbh, fbl, base_ref, vh, vl, acc, kr, extra, copies, sems = refs
    where = Rows(rows, xor)
    pairs = rows * SUB // 2
    near = nbh.shape[0]
    shift = real_ref[0:1, :]
    shift = jnp.concatenate([shift, shift], 1)

    def bands(s, i):
        if xor and s >= near:
            return (fbh, fbl)[i], s - near
        return (nbh, nbl)[i], s

    blank = jnp.zeros((2, 16, 2 * LANES), BF16)
    for ref in (vh, vl):
        ref[0:2] = blank
        ref[pairs + 2 : pairs + 4] = blank
    inside = where.inside()

    acc[0 : near * 8 + 4] = nacc[...]
    if ntiles:
        acc[near * 8 + 4 :] = jnp.zeros((pairs - near * 8, 16, 2 * LANES), F32)
        blocks = [where.block(near + k) - near for k in range(len(tiles))]
        high, low, _ = tables(taps_ref, radius_ref)
        lines = [labels[j : j + 1, :] for j in range(ntiles)]
        make_bands(where, blocks, high, low, lines, halo, base_ref, fbh, fbl)
        make_window(where, blocks, tiles, halo, uh, ul)
        for s in range(near, rows):
            spread_rows(bands, uh, ul, near, acc, s)

    def finish(n, count):
        def body(s):
            start = s * 8
            value = acc[pl.ds(start + 2, 8)]
            if n > 0:
                value = value - shift * kr[n - 1, pl.ds(start, 8)]
            value = value * inside[None]
            kr[n, pl.ds(start, 8)] = value
            high, low = split(value)
            vh[pl.ds(start + 2, 8)] = high
            vl[pl.ds(start + 2, 8)] = low

        where.each(body, count)

    def forward(first, count, last):
        def body(s):
            total = gather_rows(bands, vh, vl, s)
            if last:
                kr[NB - 1, pl.ds(s * 8, 8)] = total
            for ref, value in zip((uh, ul), split(total)):
                ref[pl.ds(s * 8, 8)] = value

        where.each(body, count, first)

    fewer = rows - 1
    finish(0, rows)
    for n, first, into, out in ((1, 1, rows, rows), (2, 0, fewer, fewer)):
        forward(first, into, False)
        if n == 1 and xor:
            acc[0:12] = nacc1[...]
            acc[12:] = jnp.zeros((pairs - 8, 16, 2 * LANES), F32)
        else:
            acc[...] = jnp.zeros_like(acc)
        where.each(lambda s: spread_rows(bands, uh, ul, 0, acc, s), into, first)
        finish(n, out)
    forward(0, fewer, True)

    for side, (ref, row) in enumerate(zip((keep_ref, send_ref), where.own())):
        for n in range(NB):
            for p in range(8):
                value = halves(kr[n, row * 8 + p])
                if n < NB - 1:
                    ref[n, p] = value
                else:
                    extra[side, p] = value
    gram = jnp.zeros((NB * 16, NB * 16), F32)
    for p in range(8):
        stack = [
            jnp.concatenate([ref[n, p] for n in range(NB - 1)] + [extra[side, p]], 0)
            for side, ref in enumerate((keep_ref, send_ref))
        ]
        stack = jnp.concatenate(stack, 1)
        gram = gram + lax.dot_general(stack, stack, NT, precision=HIGHEST, preferred_element_type=F32)
    gram = jnp.concatenate([gram, jnp.zeros_like(gram)], 1)
    lanes, sub = lane_iota(16), lax.broadcasted_iota(jnp.int32, (16, LANES), 0)
    rel = lanes & 15

    def moved(i, j, a):
        return pltpu.roll(gram[16 * i : 16 * i + 16], (16 * (a - j)) % LANES, 1)

    message = jnp.zeros((16, LANES), F32)
    for a in range(NB - 1):
        even = moved(a, a, a)
        odd = moved(a, a + 1, a) if a < NB - 2 else moved(a + 1, a + 1, a) - shift[:, :LANES] * even
        here = lanes >> 4 == a
        message = jnp.where(here, jnp.where(sub >= rel, even, odd), message)
        corner = jnp.sum(jnp.where(here & (sub == rel), odd, 0.0), axis=1, keepdims=True)
        message = jnp.where(lanes == 48 + a, corner, message)
    message = jnp.where(lanes[:8] < LANES // 2, message[:8], pltpu.roll(message[8:], LANES // 2, 1))
    share = copies.shape[0]
    for dev in range(share):
        copies[dev] = message
    moves = [
        pltpu.make_async_copy(copies, gram_ref.at[pl.ds(i * share, share)], sems.at[i])
        for i in range(ndev // share)
    ]
    for move in moves:
        move.start()
    for move in moves:
        move.wait()


def last_kernel(rows, xor, real_ref, nbh, nbl, fbh, fbl, uh, ul, keep_ref, send_ref, keep3, send3, acc):
    where = Rows(rows, xor)
    near = nbh.shape[0]
    acc[...] = jnp.zeros_like(acc)
    bands = lambda s, i: ((nbh, nbl)[i], s)
    where.each(lambda s: spread_rows(bands, uh, ul, 0, acc, s), near)
    if xor:
        wh, wl = (stage_weights(ref, 0, True) for ref in (fbh, fbl))
        high = uh[near * 8 : near * 8 + 2].reshape(32, 2 * LANES)
        low = ul[near * 8 : near * 8 + 2].reshape(32, 2 * LANES)
        for t in (3, 4):
            out = product(high, low, wh[t], wl[t], NN).reshape(2, 16, 2 * LANES)
            acc[near * 8 + 4 - t : near * 8 + 6 - t] += out
    for ref, old, row in zip((keep3, send3), (keep_ref, send_ref), where.own()):
        for p in range(8):
            ref[p] = halves(acc[row * 8 + 2 + p]) - real_ref[0:1, :] * old[NB - 2, p]


def final_kernel(
    ndev, xor, real_ref, gram_ref, keep_ref, keep3, other_ref, other3, solution_ref, residual_ref
):
    r, q, _ = place()
    damp = real_ref[0:1, :] + 0.25 * DAMPING
    parts = [gram_ref[dev] for dev in range(ndev)]
    while len(parts) > 1:
        parts = [a + b for a, b in zip(parts[::2], parts[1::2])]
    lanes, sub = lane_iota(16), lax.broadcasted_iota(jnp.int32, (16, LANES), 0)
    shared = jnp.concatenate([parts[0], pltpu.roll(parts[0], LANES // 2, 1)], 0)
    turned = jnp.concatenate([shared] + [jnp.zeros_like(shared)] * 7, 0).T
    grams = []
    for a in range(NB - 1):
        block = pltpu.roll(shared, LANES - 16 * a, 1) if a else shared
        other = turned[16 * a : 16 * a + 16]
        corner = shared[:, 48 + a : 49 + a]
        grams.append(jnp.where(sub >= lanes, block, other))
        grams.append(jnp.where(sub < lanes, block, jnp.where(sub == lanes, corner, other)))

    def at(g, place):
        return pltpu.roll(grams[g], 16 * place, 1) if place else grams[g]

    lines = []
    for i in range(3):
        line = jnp.zeros((16, LANES), F32)
        for j in range(3):
            line = jnp.where(lanes >> 4 == j, at(i + j + 1, j) + damp * at(i + j, j), line)
        lines.append(jnp.where(lanes >> 4 == 3, at(i, 3), line))
    matrix = jnp.concatenate(lines, 0)
    index = lax.broadcasted_iota(jnp.int32, (48, LANES), 0)
    for panel in range(6):
        spread = [
            jnp.broadcast_to(matrix[:, 8 * panel + i : 8 * panel + i + 1], (48, LANES)) for i in range(8)
        ]
        for i in range(8):
            k = 8 * panel + i
            column = spread[i]
            inverse = 1.0 / column[k : k + 1, :]
            row = matrix[k : k + 1, :] * inverse
            scaled = column - (index == k).astype(F32)
            matrix = matrix - scaled * row
            for j in range(i + 1, 8):
                m = 8 * panel + j
                spread[j] = spread[j] - scaled * (column[m : m + 1, :] * inverse)
    c = [pltpu.roll(matrix[16 * i : 16 * i + 16], LANES - 48, 1) for i in range(3)]
    eye = (lax.broadcasted_iota(jnp.int32, (16, LANES), 0) == lanes).astype(F32)
    zero = jnp.zeros((16, LANES), F32)
    in_solution = [0.5 * c[0], 0.5 * c[1], 0.5 * c[2], zero]
    in_residual = [
        2.0 * (eye - damp * c[0]),
        -2.0 * (c[0] + damp * c[1]),
        -2.0 * (c[1] + damp * c[2]),
        -2.0 * c[2],
    ]
    weights = jnp.concatenate(
        [jnp.where(lanes < 16, a, pltpu.roll(b, 16, 1)) for a, b in zip(in_solution, in_residual)], 0
    )
    weights = jnp.concatenate([weights, jnp.zeros_like(weights)], 0).T[:32, : NB * 16]
    first = lanes < LANES // 2
    first2 = jnp.concatenate([first, first], 0)
    outs = (
        solution_ref.reshape(16 * SUB, LANES),
        residual_ref.reshape(16 * SUB, LANES),
    )
    for p in range(8):
        mine = jnp.concatenate([keep_ref[n, p] for n in range(NB - 1)] + [keep3[p]], 0)
        pair = jnp.concatenate([other_ref[n, p] for n in range(NB - 1)] + [other3[p]], 0)
        both = jnp.concatenate([mine, pair], 1)
        out = lax.dot_general(weights, both, NN, precision=HIGHEST, preferred_element_type=F32)
        a, b = out[:, :LANES], out[:, LANES:]
        left, right = jnp.where(q == 0, a, b), jnp.where(q == 0, b, a)
        even = jnp.where(first2, left, pltpu.roll(right, LANES // 2, 1))
        odd = jnp.where(first2, pltpu.roll(left, LANES // 2, 1), right)
        for i, line in ((2 * p, even), (2 * p + 1, odd)):
            i = i + (r >> 1) * (SUB - 1 - 2 * i) if xor else i
            for o, ref in enumerate(outs):
                ref[pl.ds(i, 16, stride=SUB), :] = line[16 * o : 16 * o + 16]


def per_device(measured, regions, kernels, radius):
    nrow, ncol = lax.axis_size("row"), lax.axis_size("col")
    ndev = nrow * ncol
    def flip(value, bit):
        return lax.ppermute(value, "row", [(i, i ^ bit) for i in range(nrow)])

    facing = []
    for i in range(nrow):
        for j in range(ncol):
            other = j + (1 if (i ^ j) & 1 else -1)
            if 0 <= other < ncol:
                facing.append((i * ncol + j, i * ncol + other))

    def call(kernel, name, out, operands, scratch, mib, specs=None):
        return pl.pallas_call(
            kernel,
            out_shape=[jax.ShapeDtypeStruct(shape, kind) for shape, kind in out],
            in_specs=[VMEM] * len(operands),
            out_specs=specs or [VMEM] * len(out),
            scratch_shapes=[pltpu.VMEM(*s) if isinstance(s, tuple) else s for s in scratch],
            compiler_params=params(mib),
            name=name,
        )(*operands)

    def bands_of(count):
        return ((count, K, LANES, LANES), BF16)

    def rows_of(count, kind):
        return ((count, 16, 2 * LANES), kind)

    def bases_of(count):
        return ((count, K, 8, LANES), F32)

    def edges_of(count):
        return ((count * (SUB // PACK), 16, LANES), F32)

    xor = nrow == 4
    if xor:
        mine = measured[None]
        tiles = [mine, flip(mine, 1)]
        labels = [regions, flip(regions, 1)]
        over = flip(mine, 2)
    else:
        tiles = [lax.all_gather(measured, "row", axis=0)]
        labels = [lax.all_gather(regions, "row", axis=0, tiled=True)]
    near, pairs = sum(t.shape[0] for t in tiles), nrow * SUB // 2
    edges, reach = call(
        first_kernel,
        "first",
        [edges_of(tiles[0].shape[0]), ((8, LANES), jnp.int32)],
        [tiles[0], radius[None]],
        [],
        4,
    )
    slots = edges_of(near)[0][0] + 1
    edges, tags = call(
        functools.partial(pack_kernel, len(labels)),
        "pack",
        [((slots, 16, LANES), F32), ((16, LANES), F32)],
        [edges, *labels, *tiles[1:]],
        [],
        4,
    )
    halo = lax.ppermute(edges, ("row", "col"), facing)
    taps = jnp.transpose(kernels, (1, 2, 0))
    nbh, nbl, nacc, nacc1, real = call(
        functools.partial(near_kernel, nrow, xor, len(tiles)),
        "near",
        [bands_of(near)] * 2 + [rows_of(near * 8 + 4, F32), rows_of(12, F32), ((8, LANES), F32)],
        [taps, reach, tags, halo, *tiles],
        [bases_of(near)] + [rows_of(near * 8, BF16)] * 2 + [rows_of(12, BF16)] * 2,
        8 + 2 * nrow,
    )
    far, ntiles = [], 0
    if xor:
        over, halo, tags = lax.optimization_barrier((over, halo, tags))
        far, ntiles = [flip(tags, 2), flip(halo, 2), over, flip(over, 1)], 2
    packed = ((NB - 1, 8, 16, LANES), F32)
    extra = max(nrow - near, 1)
    share = max(ndev // 8, 1)
    out = [((ndev, 8, LANES), F32), packed, packed] + [rows_of(pairs, BF16)] * 2 + [bands_of(extra)] * 2
    grams, keep, send, uh, ul, fbh, fbl = call(
        functools.partial(main_kernel, nrow, xor, ndev, ntiles),
        "krylov",
        out,
        [taps, reach, real, nbh, nbl, nacc, nacc1, *far],
        [bases_of(extra)]
        + [rows_of(pairs + 4, BF16)] * 2
        + [rows_of(pairs + 4, F32), ((NB, pairs, 16, 2 * LANES), F32), ((2, 8, 16, LANES), F32)]
        + [((share, 8, LANES), F32), pltpu.SemaphoreType.DMA((ndev // share,))],
        8 + 3 * nrow,
        [pl.BlockSpec(memory_space=pl.ANY)] + [VMEM] * (len(out) - 1),
    )
    grams = lax.all_to_all(grams, ("row", "col"), 0, 0)
    single = ((8, 16, LANES), F32)
    keep3, send3 = call(
        functools.partial(last_kernel, nrow, xor),
        "last",
        [single, single],
        [real, nbh, nbl, fbh, fbl, uh, ul, keep, send],
        [rows_of(near * 8 + 4, F32)],
        8 + 2 * nrow,
    )
    send, send3 = lax.optimization_barrier((send, send3))
    tile = ((16, SUB, LANES), F32)
    return tuple(
        call(
            functools.partial(final_kernel, ndev, xor),
            "combine",
            [tile, tile],
            [real, grams, keep, keep3, flip(send, 1), flip(send3, 1)],
            [],
            8,
        )
    )


def solution(mesh):
    in_specs = (P(None, "row", "col"), P("row", "col"), P(), P())
    out_specs = (P(None, "row", "col"), P(None, "row", "col"))
    return jax.shard_map(
        per_device, mesh=mesh, in_specs=in_specs, out_specs=out_specs, check_vma=False
    )
```

profile of v0, /device:TPU:0, one launch (start us, length us, event | category | flops | bytes accessed | tf_op | source)
XLA Modules:
  0.0 40.0 jit_solution(17638118993087834079)
XLA Ops:
  0.6 0.0 copy-start.4
  0.6 0.0 copy-start.3
  0.6 0.5 %collective-permute-start.1 = (f32[1,16,16,128]{3,2,1,0:T(8,128)}, f32[1,16,16,128]{3,2,1,0:T(8,128)S(1)}, u32[]{:S(2)}, u32[]{:S(2)}) collective-permute-start(f32[1,16,16,128]{3,2,1,0:T(8,128)} %bitcast.3), channel_id=1, source_target_pairs={{0,8},{8,0},{16,24},{24,16},{1,9},{9,1},{17,25},{25,17},{2,10},{10... | collective-permute-start | bytes 393224 | tf_op jit(solution)/shard_map/ppermute | solution.py:480
  1.2 2.6 %collective-permute-start.3 = (f32[1,16,16,128]{3,2,1,0:T(8,128)}, f32[1,16,16,128]{3,2,1,0:T(8,128)S(1)}, u32[]{:S(2)}, u32[]{:S(2)}) collective-permute-start(f32[1,16,16,128]{3,2,1,0:T(8,128)} %bitcast.4), channel_id=1, source_target_pairs={{0,16},{8,24},{16,0},{24,8},{1,17},{9,25},{17,1},{25,9},{2,18},{10... | collective-permute-start | bytes 393224 | tf_op jit(solution)/shard_map/ppermute | solution.py:480
  3.7 0.0 copy-done.4
  3.7 0.2 collective-permute-start
  3.9 0.0 copy-done.3
  3.9 0.0 copy-start
  3.9 0.9 %copy-done = f32[16,16,128]{2,1,0:T(8,128)S(1)} copy-done((f32[16,16,128]{2,1,0:T(8,128)S(1)}, f32[16,16,128]{2,1,0:T(8,128)}, u32[]{:S(2)}) %copy-start) | copy-done | bytes 131096
  4.8 0.0 copy-start.1
  4.8 0.1 first.1
  4.9 0.0 collective-permute-done.refs_1_
  4.9 0.0 collective-permute-done.1.refs_2_.refs_1_
  4.9 0.0 copy-start.2
  5.0 0.1 pack.1
  5.1 0.7 %collective-permute-start.2 = (f32[9,16,128]{2,1,0:T(8,128)S(1)}, f32[9,16,128]{2,1,0:T(8,128)S(1)}, u32[]{:S(2)}, u32[]{:S(2)}) collective-permute-start(f32[9,16,128]{2,1,0:T(8,128)S(1)} %get-tuple-element.28), channel_id=1, source_target_pairs={{1,2},{2,1},{3,4},{4,3},{5,6},{6,5},{8,9},{9,8},{10,11},{11,10},{1... | collective-permute-start | bytes 221192 | tf_op jit(solution)/shard_map/ppermute | solution.py:539
  5.7 2.3 %collective-permute-done.3.refs_2_ = f32[1,16,16,128]{3,2,1,0:T(8,128)S(1)} collective-permute-done((f32[1,16,16,128]{3,2,1,0:T(8,128)}, f32[1,16,16,128]{3,2,1,0:T(8,128)S(1)}, u32[]{:S(2)}, u32[]{:S(2)}) %collective-permute-start.3) | collective-permute-done | bytes 131104 | tf_op jit(solution)/shard_map/ppermute | solution.py:480
  8.0 0.0 collective-permute-done.2.halo
  8.0 2.5 %collective-permute-start.6 = (f32[1,16,16,128]{3,2,1,0:T(8,128)S(1)}, f32[1,16,16,128]{3,2,1,0:T(8,128)S(1)}, u32[]{:S(2)}, u32[]{:S(2)}) collective-permute-start(f32[1,16,16,128]{3,2,1,0:T(8,128)S(1)} %collective-permute-done.3.refs_2_), channel_id=1, source_target_pairs={{0,8},{8,0},{16,24},{24,16},{1,9},{9,1},{17,25},{25,17},{2,10},{10... | collective-permute-start | bytes 393224 | tf_op jit(solution)/shard_map/ppermute | solution.py:480
  10.5 0.5 %collective-permute-start.5 = (f32[9,16,128]{2,1,0:T(8,128)S(1)}, f32[9,16,128]{2,1,0:T(8,128)S(1)}, u32[]{:S(2)}, u32[]{:S(2)}) collective-permute-start(f32[9,16,128]{2,1,0:T(8,128)S(1)} %collective-permute-done.2.halo), channel_id=1, source_target_pairs={{0,16},{8,24},{16,0},{24,8},{1,17},{9,25},{17,1},{25,9},{2,18},{10... | collective-permute-start | bytes 221192 | tf_op jit(solution)/shard_map/ppermute | solution.py:480
  11.0 1.5 %collective-permute-start.4 = (f32[16,128]{1,0:T(8,128)S(1)}, f32[16,128]{1,0:T(8,128)S(1)}, u32[]{:S(2)}, u32[]{:S(2)}) collective-permute-start(f32[16,128]{1,0:T(8,128)S(1)} %get-tuple-element.34.labels), channel_id=1, source_target_pairs={{0,16},{8,24},{16,0},{24,8},{1,17},{9,25},{17,1},{25,9},{2,18},{10... | collective-permute-start | bytes 24584 | tf_op jit(solution)/shard_map/ppermute | solution.py:480
  12.5 0.0 copy-done.1
  12.5 0.0 copy-done.2
  12.5 2.9 %near.1 = (bf16[2,9,128,128]{3,2,1,0:T(8,128)(2,1)S(1)}, bf16[2,9,128,128]{3,2,1,0:T(8,128)(2,1)S(1)}, f32[20,16,256]{2,1,0:T(8,128)S(1)}, f32[12,16,256]{2,1,0:T(8,128)S(1)}, f32[8,128]{1,0:T(8,128)S(1)}) custom-call(f32[9,9,64]{2,1,0:T(8,128)S(1)} %bitcast.7, s32[8,128]{1,0:T(8,128)S(1)} %get-tuple-element.25.radius_ref, ...), custom_call_target="tpu_custom_call" | custom-call | tf_op jit(solution)/shard_map/near/pallas_call | solution.py:490
  15.4 0.0 collective-permute-done.4.refs_0_
  15.4 0.0 collective-permute-done.5.refs_1_
  15.4 0.0 collective-permute-done.6.refs_3_
  15.5 8.0 %krylov.1 = (f32[32,8,128]{2,1,0:T(8,128)}, f32[3,8,16,128]{3,2,1,0:T(8,128)S(1)}, f32[3,8,16,128]{3,2,1,0:T(8,128)S(1)}, bf16[32,16,256]{2,1,0:T(8,128)(2,1)S(1...) custom-call(f32[9,9,64]{2,1,0:T(8,128)S(1)} %bitcast.8, ...), custom_call_target="tpu_custom_call" | custom-call | tf_op jit(solution)/shard_map/krylov/pallas_call | solution.py:490
  23.5 5.9 %all-to-all-start = ((f32[32,8,128]{2,1,0:T(8,128)}), f32[32,8,128]{2,1,0:T(8,128)S(1)}, u32[]{:S(2)}, u32[]{:S(2)}) async-start(f32[32,8,128]{2,1,0:T(8,128)} %get-tuple-element.37), calls=%async_computation | async-start | bytes 262144 | tf_op jit(solution)/shard_map/all_to_all | solution.py:569
  29.4 0.9 %last.1 = (f32[8,16,128]{2,1,0:T(8,128)S(1)}, f32[8,16,128]{2,1,0:T(8,128)S(1)}) custom-call(f32[8,128]{1,0:T(8,128)S(1)} %get-tuple-element.29.real_ref, bf16[2,9,128,128]{3,2,1,0:T(8,128)(2,1)S(1)} %get-tuple-element.30.nbh, bf16[2,9,128,128]{3,2,1,0:T(8,128)(2,1)S(1)} %get-tuple-element.31.nbl, bf16[2,9,128,128]{3,2,1,0:T(8,128)(2,1)S(1)} %get-tuple-element.39.fbh, ...), custom_call_target="tpu_custom_call" | custom-call | tf_op jit(solution)/shard_map/last/pallas_call | solution.py:490
  30.2 0.3 collective-permute-start.7
  30.5 0.3 collective-permute-start.8
  30.8 1.0 %collective-permute-done.8.other3 = f32[8,16,128]{2,1,0:T(8,128)S(1)} collective-permute-done((f32[8,16,128]{2,1,0:T(8,128)S(1)}, f32[8,16,128]{2,1,0:T(8,128)S(1)}, u32[]{:S(2)}, u32[]{:S(2)}) %collective-permute-start.8) | collective-permute-done | bytes 65568 | tf_op jit(solution)/shard_map/ppermute | solution.py:480
  31.8 0.0 collective-permute-done.7.other_ref
  31.8 5.3 %all-to-all-done.gram_ref = f32[32,8,128]{2,1,0:T(8,128)S(1)} async-done(((f32[32,8,128]{2,1,0:T(8,128)}), f32[32,8,128]{2,1,0:T(8,128)S(1)}, u32[]{:S(2)}, u32[]{:S(2)}) %all-to-all-start) | async-done | bytes 131104 | tf_op jit(solution)/shard_map/all_to_all | solution.py:569
  37.1 2.9 %combine.1 = (f32[16,16,128]{2,1,0:T(8,128)}, f32[16,16,128]{2,1,0:T(8,128)}) custom-call(f32[8,128]{1,0:T(8,128)S(1)} %get-tuple-element.29.real_ref, f32[32,8,128]{2,1,0:T(8,128)S(1)} %all-to-all-done.gram_ref, f32[3,8,16,128]{3,2,1,0:T(8,128)S(1)} %get-tuple-element.38.keep_ref, f32[8,16,128]{2,1,0:T(8,128)S(1)} %get-tuple-element.44.keep3, ...), custom_call_target="tpu_custom_call" | custom-call | tf_op jit(solution)/shard_map/combine/pallas_call | solution.py:490
Async XLA Ops:
  0.6 3.1 %copy-start.4 = (s32[1,8]{1,0:T(1,128)S(1)}, s32[1,8]{1,0:T(1,128)}, u32[]{:S(2)}) copy-start(s32[1,8]{1,0:T(1,128)} %refs_0_.1) | copy-start | bytes 100
  0.6 3.3 %copy-start.3 = (s32[64]{0:T(128)S(1)}, s32[64]{0:T(128)}, u32[]{:S(2)}) copy-start(s32[64]{0:T(128)} %param.7) | copy-start | bytes 772
  0.6 4.3 %collective-permute-start.1 = (f32[1,16,16,128]{3,2,1,0:T(8,128)}, f32[1,16,16,128]{3,2,1,0:T(8,128)S(1)}, u32[]{:S(2)}, u32[]{:S(2)}) collective-permute-start(f32[1,16,16,128]{3,2,1,0:T(8,128)} %bitcast.3), channel_id=1, source_target_pairs={{0,8},{8,0},{16,24},{24,16},{1,9},{9,1},{17,25},{25,17},{2,10},{10... | collective-permute-start | bytes 393224 | tf_op jit(solution)/shard_map/ppermute | solution.py:480
  1.2 6.9 %collective-permute-start.3 = (f32[1,16,16,128]{3,2,1,0:T(8,128)}, f32[1,16,16,128]{3,2,1,0:T(8,128)S(1)}, u32[]{:S(2)}, u32[]{:S(2)}) collective-permute-start(f32[1,16,16,128]{3,2,1,0:T(8,128)} %bitcast.4), channel_id=1, source_target_pairs={{0,16},{8,24},{16,0},{24,8},{1,17},{9,25},{17,1},{25,9},{2,18},{10... | collective-permute-start | bytes 393224 | tf_op jit(solution)/shard_map/ppermute | solution.py:480
  3.7 1.2 %collective-permute-start = (s32[1,8]{1,0:T(1,128)S(1)}, s32[1,8]{1,0:T(1,128)S(1)}, u32[]{:S(2)}, u32[]{:S(2)}) collective-permute-start(s32[1,8]{1,0:T(1,128)S(1)} %copy-done.4), channel_id=1, source_target_pairs={{0,8},{8,0},{16,24},{24,16},{1,9},{9,1},{17,25},{25,17},{2,10},{10... | collective-permute-start | bytes 104 | tf_op jit(solution)/shard_map/ppermute | solution.py:480
  3.9 0.9 %copy-start = (f32[16,16,128]{2,1,0:T(8,128)S(1)}, f32[16,16,128]{2,1,0:T(8,128)}, u32[]{:S(2)}) copy-start(f32[16,16,128]{2,1,0:T(8,128)} %param.4) | copy-start | bytes 393220
  4.8 7.7 %copy-start.1 = (f32[16,16,128]{2,1,0:T(8,128)S(1)}, f32[16,16,128]{2,1,0:T(8,128)}, u32[]{:S(2)}) copy-start(f32[16,16,128]{2,1,0:T(8,128)} %param.4) | copy-start | bytes 393220
  4.9 7.6 %copy-start.2 = (f32[64,9,9]{0,2,1:T(8,128)S(1)}, f32[64,9,9]{0,2,1:T(8,128)}, u32[]{:S(2)}) copy-start(f32[64,9,9]{0,2,1:T(8,128)} %param.6) | copy-start | bytes 62212
  5.1 3.0 %collective-permute-start.2 = (f32[9,16,128]{2,1,0:T(8,128)S(1)}, f32[9,16,128]{2,1,0:T(8,128)S(1)}, u32[]{:S(2)}, u32[]{:S(2)}) collective-permute-start(f32[9,16,128]{2,1,0:T(8,128)S(1)} %get-tuple-element.28), channel_id=1, source_target_pairs={{1,2},{2,1},{3,4},{4,3},{5,6},{6,5},{8,9},{9,8},{10,11},{11,10},{1... | collective-permute-start | bytes 221192 | tf_op jit(solution)/shard_map/ppermute | solution.py:539
  8.0 7.4 %collective-permute-start.6 = (f32[1,16,16,128]{3,2,1,0:T(8,128)S(1)}, f32[1,16,16,128]{3,2,1,0:T(8,128)S(1)}, u32[]{:S(2)}, u32[]{:S(2)}) collective-permute-start(f32[1,16,16,128]{3,2,1,0:T(8,128)S(1)} %collective-permute-done.3.refs_2_), channel_id=1, source_target_pairs={{0,8},{8,0},{16,24},{24,16},{1,9},{9,1},{17,25},{25,17},{2,10},{10... | collective-permute-start | bytes 393224 | tf_op jit(solution)/shard_map/ppermute | solution.py:480
  10.5 4.9 %collective-permute-start.5 = (f32[9,16,128]{2,1,0:T(8,128)S(1)}, f32[9,16,128]{2,1,0:T(8,128)S(1)}, u32[]{:S(2)}, u32[]{:S(2)}) collective-permute-start(f32[9,16,128]{2,1,0:T(8,128)S(1)} %collective-permute-done.2.halo), channel_id=1, source_target_pairs={{0,16},{8,24},{16,0},{24,8},{1,17},{9,25},{17,1},{25,9},{2,18},{10... | collective-permute-start | bytes 221192 | tf_op jit(solution)/shard_map/ppermute | solution.py:480
  11.0 4.4 %collective-permute-start.4 = (f32[16,128]{1,0:T(8,128)S(1)}, f32[16,128]{1,0:T(8,128)S(1)}, u32[]{:S(2)}, u32[]{:S(2)}) collective-permute-start(f32[16,128]{1,0:T(8,128)S(1)} %get-tuple-element.34.labels), channel_id=1, source_target_pairs={{0,16},{8,24},{16,0},{24,8},{1,17},{9,25},{17,1},{25,9},{2,18},{10... | collective-permute-start | bytes 24584 | tf_op jit(solution)/shard_map/ppermute | solution.py:480
  23.5 13.6 %all-to-all-start = ((f32[32,8,128]{2,1,0:T(8,128)}), f32[32,8,128]{2,1,0:T(8,128)S(1)}, u32[]{:S(2)}, u32[]{:S(2)}) async-start(f32[32,8,128]{2,1,0:T(8,128)} %get-tuple-element.37), calls=%async_computation | async-start | bytes 262144 | tf_op jit(solution)/shard_map/all_to_all | solution.py:569
  30.2 1.6 %collective-permute-start.7 = (f32[3,8,16,128]{3,2,1,0:T(8,128)S(1)}, f32[3,8,16,128]{3,2,1,0:T(8,128)S(1)}, u32[]{:S(2)}, u32[]{:S(2)}) collective-permute-start(f32[3,8,16,128]{3,2,1,0:T(8,128)S(1)} %get-tuple-element.46.send_ref), channel_id=1, source_target_pairs={{0,8},{8,0},{16,24},{24,16},{1,9},{9,1},{17,25},{25,17},{2,10},{10... | collective-permute-start | bytes 589832 | tf_op jit(solution)/shard_map/ppermute | solution.py:480
  30.5 1.3 %collective-permute-start.8 = (f32[8,16,128]{2,1,0:T(8,128)S(1)}, f32[8,16,128]{2,1,0:T(8,128)S(1)}, u32[]{:S(2)}, u32[]{:S(2)}) collective-permute-start(f32[8,16,128]{2,1,0:T(8,128)S(1)} %get-tuple-element.47), channel_id=1, source_target_pairs={{0,8},{8,0},{16,24},{24,16},{1,9},{9,1},{17,25},{25,17},{2,10},{10... | collective-permute-start | bytes 196616 | tf_op jit(solution)/shard_map/ppermute | solution.py:480
where the time goes:
time: 40.2 us; the launch traced here: 40 us
  Pallas kernels  14.9 us (37%)
  starting transfers between devices  14.8 us (37%)
  waiting for transfers between devices  8.6 us (21%)
  local copies, waits for them, and re-layouts  0.92 us (2%)
  between operations  0.75 us (2%)
    pallas_call x6, Pallas kernels, call(): pl.pallas_call(kernel, out_shape=[jax.ShapeDtypeStruct(shape, kind) for s...  14.9 us
    ppermute x8, starting transfers between devices, flip(): return lax.ppermute(value, 'row', [(i, i ^ bit) for i in range(nrow)])  8.32 us
    all_to_all x1, starting transfers between devices, per_device(): grams = lax.all_to_all(grams, ('row', 'col'), 0, 0)  5.86 us
    all_to_all x1, waiting for transfers between devices, per_device(): grams = lax.all_to_all(grams, ('row', 'col'), 0, 0)  5.26 us
    ppermute x8, waiting for transfers between devices, flip(): return lax.ppermute(value, 'row', [(i, i ^ bit) for i in range(nrow)])  3.33 us
    unnamed x10, local copies, waits for them, and re-layouts  0.92 us
  transfers between devices with their start and end apart: 10, of which 3 were waited for; matrix products, arithmetic and copies ran while one was open for 0% of the time, Pallas kernels for 10%

commit v1 on v0

--- a/solution.py
+++ b/solution.py
@@ -22,7 +22,6 @@
 BF16 = jnp.bfloat16
 NN = (((1,), (0,)), ((), ()))
 NT = (((1,), (1,)), ((), ()))
-HIGHEST = lax.Precision.HIGHEST
 VMEM = pl.BlockSpec(memory_space=pltpu.VMEM)
 SMEM = pl.BlockSpec(memory_space=pltpu.SMEM)
 def params(mib):
@@ -187,8 +186,12 @@
     for j, (s, (ref, index)) in enumerate(zip(blocks, tiles)):
         for p in range(SUB // 2):
             parts = []
-            for i in (where.turn(2 * p, SUB - 1), where.turn(2 * p + 1, SUB - 1)):
-                line = pltpu.roll(row_of(ref, index, i), HALO + (LANES - 2 * HALO) * where.q, 1)
+            for row in (2 * p, 2 * p + 1):
+                i = where.turn(row, SUB - 1)
+                line = row_of(ref, index, row)
+                if where.xor:
+                    line = jnp.where(where.down > 0, row_of(ref, index, SUB - 1 - row), line)
+                line = pltpu.roll(line, HALO + (LANES - 2 * HALO) * where.q, 1)
                 edge = halo[j * (SUB // PACK) + i // PACK]
                 edge = pltpu.roll(edge, (LANES - HALO * (i % PACK) + (LANES - HALO) * where.q) % LANES, 1)
                 parts.append(jnp.where(where.in_halo, edge, line))
@@ -200,6 +203,36 @@
     both = lax.dot_general(jnp.concatenate([high, low], 0), wh, dims, preferred_element_type=F32)
     third = lax.dot_general(high, wl, dims, preferred_element_type=F32)
     return both[: high.shape[0]] + both[high.shape[0] :] + third
+
+
+def three(value):
+    parts = []
+    for _ in range(3):
+        parts.append(value.astype(BF16))
+        value = value - parts[-1].astype(F32)
+    return parts
+
+
+def exact_gram(value):
+    parts = jnp.concatenate(three(value), 0)
+    out = lax.dot_general(parts, parts, NT, preferred_element_type=F32)
+    rows = value.shape[0]
+    blocks = [[out[rows * i : rows * i + rows, rows * j : rows * j + rows] for j in range(3)] for i in range(3)]
+    small = (blocks[1][1] + (blocks[0][2] + blocks[2][0])) + (blocks[1][2] + blocks[2][1])
+    return blocks[0][0] + ((blocks[0][1] + blocks[1][0]) + small)
+
+
+def exact_weights(weights):
+    high, mid, low = three(weights)
+    zero = jnp.zeros_like(high)
+    lines = ([high] * 3, [mid, mid, zero], [low, zero, zero])
+    return jnp.concatenate([jnp.concatenate(line, 1) for line in lines], 0)
+
+
+def exact_combination(weights, value):
+    out = lax.dot_general(weights, jnp.concatenate(three(value), 0), NN, preferred_element_type=F32)
+    rows = weights.shape[0] // 3
+    return out[:rows] + (out[rows : 2 * rows] + out[2 * rows :])
 
 
 def spread_rows(bands, uh, ul, base, acc, s):
@@ -346,7 +379,7 @@
             for side, ref in enumerate((keep_ref, send_ref))
         ]
         stack = jnp.concatenate(stack, 1)
-        gram = gram + lax.dot_general(stack, stack, NT, precision=HIGHEST, preferred_element_type=F32)
+        gram = gram + exact_gram(stack)
     gram = jnp.concatenate([gram, jnp.zeros_like(gram)], 1)
     lanes, sub = lane_iota(16), lax.broadcasted_iota(jnp.int32, (16, LANES), 0)
     rel = lanes & 15
@@ -416,42 +449,32 @@
     def at(g, place):
         return pltpu.roll(grams[g], 16 * place, 1) if place else grams[g]
 
-    lines = []
-    for i in range(3):
+    def line_of(entry):
         line = jnp.zeros((16, LANES), F32)
         for j in range(3):
-            line = jnp.where(lanes >> 4 == j, at(i + j + 1, j) + damp * at(i + j, j), line)
-        lines.append(jnp.where(lanes >> 4 == 3, at(i, 3), line))
-    matrix = jnp.concatenate(lines, 0)
-    index = lax.broadcasted_iota(jnp.int32, (48, LANES), 0)
+            line = jnp.where(lanes >> 4 == j, entry(j), line)
+        return line
+
+    lines = [line_of(lambda j: at(i + j + 1, j) + damp * at(i + j, j)) for i in range(3)]
+    matrix = jnp.concatenate(lines + [line_of(lambda j: at(j, j))], 0)
+    lane = lane_iota(1)
     for panel in range(6):
         spread = [
-            jnp.broadcast_to(matrix[:, 8 * panel + i : 8 * panel + i + 1], (48, LANES)) for i in range(8)
+            jnp.broadcast_to(matrix[:, 8 * panel + i : 8 * panel + i + 1], (64, LANES)) for i in range(8)
         ]
         for i in range(8):
             k = 8 * panel + i
             column = spread[i]
-            inverse = 1.0 / column[k : k + 1, :]
-            row = matrix[k : k + 1, :] * inverse
-            scaled = column - (index == k).astype(F32)
-            matrix = matrix - scaled * row
+            scaled = column * (1.0 / column[k : k + 1, :])
+            matrix = matrix - scaled * (matrix[k : k + 1, :] - (lane == k).astype(F32))
             for j in range(i + 1, 8):
                 m = 8 * panel + j
-                spread[j] = spread[j] - scaled * (column[m : m + 1, :] * inverse)
-    c = [pltpu.roll(matrix[16 * i : 16 * i + 16], LANES - 48, 1) for i in range(3)]
-    eye = (lax.broadcasted_iota(jnp.int32, (16, LANES), 0) == lanes).astype(F32)
-    zero = jnp.zeros((16, LANES), F32)
-    in_solution = [0.5 * c[0], 0.5 * c[1], 0.5 * c[2], zero]
-    in_residual = [
-        2.0 * (eye - damp * c[0]),
-        -2.0 * (c[0] + damp * c[1]),
-        -2.0 * (c[1] + damp * c[2]),
-        -2.0 * c[2],
-    ]
-    weights = jnp.concatenate(
-        [jnp.where(lanes < 16, a, pltpu.roll(b, 16, 1)) for a, b in zip(in_solution, in_residual)], 0
-    )
-    weights = jnp.concatenate([weights, jnp.zeros_like(weights)], 0).T[:32, : NB * 16]
+                spread[j] = spread[j] - scaled * column[m : m + 1, :]
+    c = jnp.where(lanes < 48, matrix[48:], 0.0)
+    eye = (sub == lanes).astype(F32)
+    weights = jnp.concatenate([0.5 * c, 2.0 * (eye - damp * c - pltpu.roll(c, 16, 1))], 0)[:, : NB * 16]
+    weights = exact_weights(weights)
+    down = r >> 1
     first = lanes < LANES // 2
     first2 = jnp.concatenate([first, first], 0)
     outs = (
@@ -459,16 +482,18 @@
         residual_ref.reshape(16 * SUB, LANES),
     )
     for p in range(8):
-        mine = jnp.concatenate([keep_ref[n, p] for n in range(NB - 1)] + [keep3[p]], 0)
-        pair = jnp.concatenate([other_ref[n, p] for n in range(NB - 1)] + [other3[p]], 0)
+        at = p + down * (7 - 2 * p) if xor else p
+        mine = jnp.concatenate([keep_ref[n, at] for n in range(NB - 1)] + [keep3[at]], 0)
+        pair = jnp.concatenate([other_ref[n, at] for n in range(NB - 1)] + [other3[at]], 0)
         both = jnp.concatenate([mine, pair], 1)
-        out = lax.dot_general(weights, both, NN, precision=HIGHEST, preferred_element_type=F32)
+        out = exact_combination(weights, both)
         a, b = out[:, :LANES], out[:, LANES:]
         left, right = jnp.where(q == 0, a, b), jnp.where(q == 0, b, a)
         even = jnp.where(first2, left, pltpu.roll(right, LANES // 2, 1))
         odd = jnp.where(first2, pltpu.roll(left, LANES // 2, 1), right)
+        if xor:
+            even, odd = jnp.where(down > 0, odd, even), jnp.where(down > 0, even, odd)
         for i, line in ((2 * p, even), (2 * p + 1, odd)):
-            i = i + (r >> 1) * (SUB - 1 - 2 * i) if xor else i
             for o, ref in enumerate(outs):
                 ref[pl.ds(i, 16, stride=SUB), :] = line[16 * o : 16 * o + 16]
 

time: 40.2 us -> 39.9 us (level)
  no operation moved by 1% of the time
where the time goes in v1:
time: 39.9 us; the launch traced here: 39.7 us
  starting transfers between devices  14.8 us (37%)
  Pallas kernels  14.6 us (37%)
  waiting for transfers between devices  8.6 us (22%)
  local copies, waits for them, and re-layouts  0.92 us (2%)
  between operations  0.75 us (2%)
    pallas_call x6, Pallas kernels, call(): pl.pallas_call(kernel, out_shape=[jax.ShapeDtypeStruct(shape, kind) for s...  14.6 us
    ppermute x8, starting transfers between devices, flip(): return lax.ppermute(value, 'row', [(i, i ^ bit) for i in range(nrow)])  8.32 us
    all_to_all x1, starting transfers between devices, per_device(): grams = lax.all_to_all(grams, ('row', 'col'), 0, 0)  5.86 us
    all_to_all x1, waiting for transfers between devices, per_device(): grams = lax.all_to_all(grams, ('row', 'col'), 0, 0)  5.26 us
    ppermute x8, waiting for transfers between devices, flip(): return lax.ppermute(value, 'row', [(i, i ^ bit) for i in range(nrow)])  3.33 us
    unnamed x10, local copies, waits for them, and re-layouts  0.92 us
  transfers between devices with their start and end apart: 10, of which 3 were waited for; matrix products, arithmetic and copies ran while one was open for 0% of the time, Pallas kernels for 10%

profile of v1, /device:TPU:0, one launch (start us, length us, event | category | flops | bytes accessed | tf_op | source)
XLA Modules:
  0.0 39.7 jit_solution(6928605614123721261)
XLA Ops:
  0.6 0.0 copy-start.4
  0.6 0.0 copy-start.3
  0.6 0.5 %collective-permute-start.1 = (f32[1,16,16,128]{3,2,1,0:T(8,128)}, f32[1,16,16,128]{3,2,1,0:T(8,128)S(1)}, u32[]{:S(2)}, u32[]{:S(2)}) collective-permute-start(f32[1,16,16,128]{3,2,1,0:T(8,128)} %bitcast.3), channel_id=1, source_target_pairs={{0,8},{8,0},{16,24},{24,16},{1,9},{9,1},{17,25},{25,17},{2,10},{10... | collective-permute-start | bytes 393224 | tf_op jit(solution)/shard_map/ppermute | solution.py:505
  1.2 2.6 %collective-permute-start.3 = (f32[1,16,16,128]{3,2,1,0:T(8,128)}, f32[1,16,16,128]{3,2,1,0:T(8,128)S(1)}, u32[]{:S(2)}, u32[]{:S(2)}) collective-permute-start(f32[1,16,16,128]{3,2,1,0:T(8,128)} %bitcast.4), channel_id=1, source_target_pairs={{0,16},{8,24},{16,0},{24,8},{1,17},{9,25},{17,1},{25,9},{2,18},{10... | collective-permute-start | bytes 393224 | tf_op jit(solution)/shard_map/ppermute | solution.py:505
  3.7 0.0 copy-done.4
  3.7 0.2 collective-permute-start
  3.9 0.0 copy-done.3
  3.9 0.0 copy-start
  3.9 0.9 %copy-done = f32[16,16,128]{2,1,0:T(8,128)S(1)} copy-done((f32[16,16,128]{2,1,0:T(8,128)S(1)}, f32[16,16,128]{2,1,0:T(8,128)}, u32[]{:S(2)}) %copy-start) | copy-done | bytes 131096
  4.8 0.0 copy-start.1
  4.8 0.1 first.1
  4.9 0.0 collective-permute-done.refs_1_
  4.9 0.0 collective-permute-done.1.refs_2_.refs_1_
  4.9 0.0 copy-start.2
  5.0 0.1 pack.1
  5.1 0.7 %collective-permute-start.2 = (f32[9,16,128]{2,1,0:T(8,128)S(1)}, f32[9,16,128]{2,1,0:T(8,128)S(1)}, u32[]{:S(2)}, u32[]{:S(2)}) collective-permute-start(f32[9,16,128]{2,1,0:T(8,128)S(1)} %get-tuple-element.28), channel_id=1, source_target_pairs={{1,2},{2,1},{3,4},{4,3},{5,6},{6,5},{8,9},{9,8},{10,11},{11,10},{1... | collective-permute-start | bytes 221192 | tf_op jit(solution)/shard_map/ppermute | solution.py:564
  5.7 2.3 %collective-permute-done.3.refs_2_ = f32[1,16,16,128]{3,2,1,0:T(8,128)S(1)} collective-permute-done((f32[1,16,16,128]{3,2,1,0:T(8,128)}, f32[1,16,16,128]{3,2,1,0:T(8,128)S(1)}, u32[]{:S(2)}, u32[]{:S(2)}) %collective-permute-start.3) | collective-permute-done | bytes 131104 | tf_op jit(solution)/shard_map/ppermute | solution.py:505
  8.0 0.0 collective-permute-done.2.halo
  8.0 2.5 %collective-permute-start.6 = (f32[1,16,16,128]{3,2,1,0:T(8,128)S(1)}, f32[1,16,16,128]{3,2,1,0:T(8,128)S(1)}, u32[]{:S(2)}, u32[]{:S(2)}) collective-permute-start(f32[1,16,16,128]{3,2,1,0:T(8,128)S(1)} %collective-permute-done.3.refs_2_), channel_id=1, source_target_pairs={{0,8},{8,0},{16,24},{24,16},{1,9},{9,1},{17,25},{25,17},{2,10},{10... | collective-permute-start | bytes 393224 | tf_op jit(solution)/shard_map/ppermute | solution.py:505
  10.5 0.5 %collective-permute-start.5 = (f32[9,16,128]{2,1,0:T(8,128)S(1)}, f32[9,16,128]{2,1,0:T(8,128)S(1)}, u32[]{:S(2)}, u32[]{:S(2)}) collective-permute-start(f32[9,16,128]{2,1,0:T(8,128)S(1)} %collective-permute-done.2.halo), channel_id=1, source_target_pairs={{0,16},{8,24},{16,0},{24,8},{1,17},{9,25},{17,1},{25,9},{2,18},{10... | collective-permute-start | bytes 221192 | tf_op jit(solution)/shard_map/ppermute | solution.py:505
  11.0 1.5 %collective-permute-start.4 = (f32[16,128]{1,0:T(8,128)S(1)}, f32[16,128]{1,0:T(8,128)S(1)}, u32[]{:S(2)}, u32[]{:S(2)}) collective-permute-start(f32[16,128]{1,0:T(8,128)S(1)} %get-tuple-element.34.labels), channel_id=1, source_target_pairs={{0,16},{8,24},{16,0},{24,8},{1,17},{9,25},{17,1},{25,9},{2,18},{10... | collective-permute-start | bytes 24584 | tf_op jit(solution)/shard_map/ppermute | solution.py:505
  12.5 0.0 copy-done.1
  12.5 0.0 copy-done.2
  12.5 2.9 %near.1 = (bf16[2,9,128,128]{3,2,1,0:T(8,128)(2,1)S(1)}, bf16[2,9,128,128]{3,2,1,0:T(8,128)(2,1)S(1)}, f32[20,16,256]{2,1,0:T(8,128)S(1)}, f32[12,16,256]{2,1,0:T(8,128)S(1)}, f32[8,128]{1,0:T(8,128)S(1)}) custom-call(f32[9,9,64]{2,1,0:T(8,128)S(1)} %bitcast.7, s32[8,128]{1,0:T(8,128)S(1)} %get-tuple-element.25.radius_ref, ...), custom_call_target="tpu_custom_call" | custom-call | tf_op jit(solution)/shard_map/near/pallas_call | solution.py:515
  15.4 0.0 collective-permute-done.4.refs_0_
  15.4 0.0 collective-permute-done.5.refs_1_
  15.4 0.0 collective-permute-done.6.refs_3_
  15.5 7.8 %krylov.1 = (f32[32,8,128]{2,1,0:T(8,128)}, f32[3,8,16,128]{3,2,1,0:T(8,128)S(1)}, f32[3,8,16,128]{3,2,1,0:T(8,128)S(1)}, bf16[32,16,256]{2,1,0:T(8,128)(2,1)S(1...) custom-call(f32[9,9,64]{2,1,0:T(8,128)S(1)} %bitcast.8, ...), custom_call_target="tpu_custom_call" | custom-call | tf_op jit(solution)/shard_map/krylov/pallas_call | solution.py:515
  23.3 5.9 %all-to-all-start = ((f32[32,8,128]{2,1,0:T(8,128)}), f32[32,8,128]{2,1,0:T(8,128)S(1)}, u32[]{:S(2)}, u32[]{:S(2)}) async-start(f32[32,8,128]{2,1,0:T(8,128)} %get-tuple-element.37), calls=%async_computation | async-start | bytes 262144 | tf_op jit(solution)/shard_map/all_to_all | solution.py:594
  29.1 0.9 %last.1 = (f32[8,16,128]{2,1,0:T(8,128)S(1)}, f32[8,16,128]{2,1,0:T(8,128)S(1)}) custom-call(f32[8,128]{1,0:T(8,128)S(1)} %get-tuple-element.29.real_ref, bf16[2,9,128,128]{3,2,1,0:T(8,128)(2,1)S(1)} %get-tuple-element.30.nbh, bf16[2,9,128,128]{3,2,1,0:T(8,128)(2,1)S(1)} %get-tuple-element.31.nbl, bf16[2,9,128,128]{3,2,1,0:T(8,128)(2,1)S(1)} %get-tuple-element.39.fbh, ...), custom_call_target="tpu_custom_call" | custom-call | tf_op jit(solution)/shard_map/last/pallas_call | solution.py:515
  30.0 0.3 collective-permute-start.7
  30.3 0.3 collective-permute-start.8
  30.6 1.0 %collective-permute-done.8.other3 = f32[8,16,128]{2,1,0:T(8,128)S(1)} collective-permute-done((f32[8,16,128]{2,1,0:T(8,128)S(1)}, f32[8,16,128]{2,1,0:T(8,128)S(1)}, u32[]{:S(2)}, u32[]{:S(2)}) %collective-permute-start.8) | collective-permute-done | bytes 65568 | tf_op jit(solution)/shard_map/ppermute | solution.py:505
  31.6 0.0 collective-permute-done.7.other_ref
  31.6 5.3 %all-to-all-done.gram_ref = f32[32,8,128]{2,1,0:T(8,128)S(1)} async-done(((f32[32,8,128]{2,1,0:T(8,128)}), f32[32,8,128]{2,1,0:T(8,128)S(1)}, u32[]{:S(2)}, u32[]{:S(2)}) %all-to-all-start) | async-done | bytes 131104 | tf_op jit(solution)/shard_map/all_to_all | solution.py:594
  36.9 2.8 %combine.1 = (f32[16,16,128]{2,1,0:T(8,128)}, f32[16,16,128]{2,1,0:T(8,128)}) custom-call(f32[8,128]{1,0:T(8,128)S(1)} %get-tuple-element.29.real_ref, f32[32,8,128]{2,1,0:T(8,128)S(1)} %all-to-all-done.gram_ref, f32[3,8,16,128]{3,2,1,0:T(8,128)S(1)} %get-tuple-element.38.keep_ref, f32[8,16,128]{2,1,0:T(8,128)S(1)} %get-tuple-element.44.keep3, ...), custom_call_target="tpu_custom_call" | custom-call | tf_op jit(solution)/shard_map/combine/pallas_call | solution.py:515
Async XLA Ops:
  0.6 3.1 %copy-start.4 = (s32[1,8]{1,0:T(1,128)S(1)}, s32[1,8]{1,0:T(1,128)}, u32[]{:S(2)}) copy-start(s32[1,8]{1,0:T(1,128)} %refs_0_.1) | copy-start | bytes 100
  0.6 3.3 %copy-start.3 = (s32[64]{0:T(128)S(1)}, s32[64]{0:T(128)}, u32[]{:S(2)}) copy-start(s32[64]{0:T(128)} %param.7) | copy-start | bytes 772
  0.6 4.3 %collective-permute-start.1 = (f32[1,16,16,128]{3,2,1,0:T(8,128)}, f32[1,16,16,128]{3,2,1,0:T(8,128)S(1)}, u32[]{:S(2)}, u32[]{:S(2)}) collective-permute-start(f32[1,16,16,128]{3,2,1,0:T(8,128)} %bitcast.3), channel_id=1, source_target_pairs={{0,8},{8,0},{16,24},{24,16},{1,9},{9,1},{17,25},{25,17},{2,10},{10... | collective-permute-start | bytes 393224 | tf_op jit(solution)/shard_map/ppermute | solution.py:505
  1.2 6.9 %collective-permute-start.3 = (f32[1,16,16,128]{3,2,1,0:T(8,128)}, f32[1,16,16,128]{3,2,1,0:T(8,128)S(1)}, u32[]{:S(2)}, u32[]{:S(2)}) collective-permute-start(f32[1,16,16,128]{3,2,1,0:T(8,128)} %bitcast.4), channel_id=1, source_target_pairs={{0,16},{8,24},{16,0},{24,8},{1,17},{9,25},{17,1},{25,9},{2,18},{10... | collective-permute-start | bytes 393224 | tf_op jit(solution)/shard_map/ppermute | solution.py:505
  3.7 1.2 %collective-permute-start = (s32[1,8]{1,0:T(1,128)S(1)}, s32[1,8]{1,0:T(1,128)S(1)}, u32[]{:S(2)}, u32[]{:S(2)}) collective-permute-start(s32[1,8]{1,0:T(1,128)S(1)} %copy-done.4), channel_id=1, source_target_pairs={{0,8},{8,0},{16,24},{24,16},{1,9},{9,1},{17,25},{25,17},{2,10},{10... | collective-permute-start | bytes 104 | tf_op jit(solution)/shard_map/ppermute | solution.py:505
  3.9 0.9 %copy-start = (f32[16,16,128]{2,1,0:T(8,128)S(1)}, f32[16,16,128]{2,1,0:T(8,128)}, u32[]{:S(2)}) copy-start(f32[16,16,128]{2,1,0:T(8,128)} %param.4) | copy-start | bytes 393220
  4.8 7.7 %copy-start.1 = (f32[16,16,128]{2,1,0:T(8,128)S(1)}, f32[16,16,128]{2,1,0:T(8,128)}, u32[]{:S(2)}) copy-start(f32[16,16,128]{2,1,0:T(8,128)} %param.4) | copy-start | bytes 393220
  4.9 7.6 %copy-start.2 = (f32[64,9,9]{0,2,1:T(8,128)S(1)}, f32[64,9,9]{0,2,1:T(8,128)}, u32[]{:S(2)}) copy-start(f32[64,9,9]{0,2,1:T(8,128)} %param.6) | copy-start | bytes 62212
  5.1 3.0 %collective-permute-start.2 = (f32[9,16,128]{2,1,0:T(8,128)S(1)}, f32[9,16,128]{2,1,0:T(8,128)S(1)}, u32[]{:S(2)}, u32[]{:S(2)}) collective-permute-start(f32[9,16,128]{2,1,0:T(8,128)S(1)} %get-tuple-element.28), channel_id=1, source_target_pairs={{1,2},{2,1},{3,4},{4,3},{5,6},{6,5},{8,9},{9,8},{10,11},{11,10},{1... | collective-permute-start | bytes 221192 | tf_op jit(solution)/shard_map/ppermute | solution.py:564
  8.0 7.4 %collective-permute-start.6 = (f32[1,16,16,128]{3,2,1,0:T(8,128)S(1)}, f32[1,16,16,128]{3,2,1,0:T(8,128)S(1)}, u32[]{:S(2)}, u32[]{:S(2)}) collective-permute-start(f32[1,16,16,128]{3,2,1,0:T(8,128)S(1)} %collective-permute-done.3.refs_2_), channel_id=1, source_target_pairs={{0,8},{8,0},{16,24},{24,16},{1,9},{9,1},{17,25},{25,17},{2,10},{10... | collective-permute-start | bytes 393224 | tf_op jit(solution)/shard_map/ppermute | solution.py:505
  10.5 4.9 %collective-permute-start.5 = (f32[9,16,128]{2,1,0:T(8,128)S(1)}, f32[9,16,128]{2,1,0:T(8,128)S(1)}, u32[]{:S(2)}, u32[]{:S(2)}) collective-permute-start(f32[9,16,128]{2,1,0:T(8,128)S(1)} %collective-permute-done.2.halo), channel_id=1, source_target_pairs={{0,16},{8,24},{16,0},{24,8},{1,17},{9,25},{17,1},{25,9},{2,18},{10... | collective-permute-start | bytes 221192 | tf_op jit(solution)/shard_map/ppermute | solution.py:505
  11.0 4.4 %collective-permute-start.4 = (f32[16,128]{1,0:T(8,128)S(1)}, f32[16,128]{1,0:T(8,128)S(1)}, u32[]{:S(2)}, u32[]{:S(2)}) collective-permute-start(f32[16,128]{1,0:T(8,128)S(1)} %get-tuple-element.34.labels), channel_id=1, source_target_pairs={{0,16},{8,24},{16,0},{24,8},{1,17},{9,25},{17,1},{25,9},{2,18},{10... | collective-permute-start | bytes 24584 | tf_op jit(solution)/shard_map/ppermute | solution.py:505
  23.3 13.6 %all-to-all-start = ((f32[32,8,128]{2,1,0:T(8,128)}), f32[32,8,128]{2,1,0:T(8,128)S(1)}, u32[]{:S(2)}, u32[]{:S(2)}) async-start(f32[32,8,128]{2,1,0:T(8,128)} %get-tuple-element.37), calls=%async_computation | async-start | bytes 262144 | tf_op jit(solution)/shard_map/all_to_all | solution.py:594
  30.0 1.6 %collective-permute-start.7 = (f32[3,8,16,128]{3,2,1,0:T(8,128)S(1)}, f32[3,8,16,128]{3,2,1,0:T(8,128)S(1)}, u32[]{:S(2)}, u32[]{:S(2)}) collective-permute-start(f32[3,8,16,128]{3,2,1,0:T(8,128)S(1)} %get-tuple-element.46.send_ref), channel_id=1, source_target_pairs={{0,8},{8,0},{16,24},{24,16},{1,9},{9,1},{17,25},{25,17},{2,10},{10... | collective-permute-start | bytes 589832 | tf_op jit(solution)/shard_map/ppermute | solution.py:505
  30.3 1.3 %collective-permute-start.8 = (f32[8,16,128]{2,1,0:T(8,128)S(1)}, f32[8,16,128]{2,1,0:T(8,128)S(1)}, u32[]{:S(2)}, u32[]{:S(2)}) collective-permute-start(f32[8,16,128]{2,1,0:T(8,128)S(1)} %get-tuple-element.47), channel_id=1, source_target_pairs={{0,8},{8,0},{16,24},{24,16},{1,9},{9,1},{17,25},{25,17},{2,10},{10... | collective-permute-start | bytes 196616 | tf_op jit(solution)/shard_map/ppermute | solution.py:505

commit v2 on v1

--- a/solution.py
+++ b/solution.py
@@ -264,6 +264,11 @@
     )
 
 
+def join_kernel(halo, tags, out):
+    out[...] = halo[...]
+    out[halo.shape[0] - 1, 8:16, :] = tags[0:8, :]
+
+
 def slots_of(tiles):
     return [(ref, index) for ref in tiles for index in range(ref.shape[0])]
 
@@ -295,9 +300,9 @@
 
 def main_kernel(rows, xor, ndev, ntiles, taps_ref, radius_ref, real_ref, nbh, nbl, nacc, nacc1, *refs):
     if ntiles:
-        labels, halo = refs[:2]
-        tiles = slots_of(refs[2 : 2 + ntiles])
-        refs = refs[2 + ntiles :]
+        halo = refs[0]
+        tiles = slots_of(refs[1 : 1 + ntiles])
+        refs = refs[1 + ntiles :]
     gram_ref, keep_ref, send_ref, uh, ul, fbh, fbl, base_ref, vh, vl, acc, kr, extra, copies, sems = refs
     where = Rows(rows, xor)
     pairs = rows * SUB // 2
@@ -321,7 +326,7 @@
         acc[near * 8 + 4 :] = jnp.zeros((pairs - near * 8, 16, 2 * LANES), F32)
         blocks = [where.block(near + k) - near for k in range(len(tiles))]
         high, low, _ = tables(taps_ref, radius_ref)
-        lines = [labels[j : j + 1, :] for j in range(ntiles)]
+        lines = [halo[halo.shape[0] - 1, 8 + j : 9 + j, :] for j in range(ntiles)]
         make_bands(where, blocks, high, low, lines, halo, base_ref, fbh, fbl)
         make_window(where, blocks, tiles, halo, uh, ul)
         for s in range(near, rows):
@@ -573,8 +578,9 @@
     )
     far, ntiles = [], 0
     if xor:
-        over, halo, tags = lax.optimization_barrier((over, halo, tags))
-        far, ntiles = [flip(tags, 2), flip(halo, 2), over, flip(over, 1)], 2
+        over, halo = lax.optimization_barrier((over, halo))
+        (joined,) = call(join_kernel, "join", [((slots, 16, LANES), F32)], [halo, tags], [], 4)
+        far, ntiles = [flip(joined, 2), over, flip(over, 1)], 2
     packed = ((NB - 1, 8, 16, LANES), F32)
     extra = max(nrow - near, 1)
     share = max(ndev // 8, 1)

time: 39.9 us -> 39.6 us (level)
  starting transfers between devices: 14.8 us -> 13.5 us
  waiting for transfers between devices: 8.6 us -> 9.26 us
    ppermute x8 -> x7, starting transfers between devices: 8.32 us -> 6.85 us  [flip(): return lax.ppermute(value, 'row', [(i, i ^ bit) for i in range(nrow)])]
    ppermute x8 -> x7, waiting for transfers between devices: 3.33 us -> 3.99 us  [flip(): return lax.ppermute(value, 'row', [(i, i ^ bit) for i in range(nrow)])]
    pallas_call x6 -> x7, Pallas kernels: 14.6 us -> 14.6 us  [call(): pl.pallas_call(kernel, out_shape=[jax.ShapeDtypeStruct(shape, kind) for s...]
  transfers between devices with their start and end apart: 10 -> 9, of which waited for: 3 -> 4; matrix products, arithmetic and copies ran while one was open for 0% -> 0% of each run, Pallas kernels for 10% -> 10%
where the time goes in v2:
time: 39.6 us; the launch traced here: 39.4 us
  Pallas kernels  14.6 us (37%)
  starting transfers between devices  13.5 us (34%)
  waiting for transfers between devices  9.26 us (23%)
  local copies, waits for them, and re-layouts  1.24 us (3%)
  between operations  0.73 us (2%)
    pallas_call x7, Pallas kernels, call(): pl.pallas_call(kernel, out_shape=[jax.ShapeDtypeStruct(shape, kind) for s...  14.6 us
    ppermute x7, starting transfers between devices, flip(): return lax.ppermute(value, 'row', [(i, i ^ bit) for i in range(nrow)])  6.85 us
    all_to_all x1, starting transfers between devices, per_device(): grams = lax.all_to_all(grams, ('row', 'col'), 0, 0)  6.01 us
    all_to_all x1, waiting for transfers between devices, per_device(): grams = lax.all_to_all(grams, ('row', 'col'), 0, 0)  5.26 us
    ppermute x7, waiting for transfers between devices, flip(): return lax.ppermute(value, 'row', [(i, i ^ bit) for i in range(nrow)])  3.99 us
    unnamed x10, local copies, waits for them, and re-layouts  1.24 us
  transfers between devices with their start and end apart: 9, of which 4 were waited for; matrix products, arithmetic and copies ran while one was open for 0% of the time, Pallas kernels for 10%

profile of v2, /device:TPU:0, one launch (start us, length us, event | category | flops | bytes accessed | tf_op | source)
XLA Modules:
  0.0 39.4 jit_solution(16847503867527004984)
XLA Ops:
  0.6 0.0 copy-start.4
  0.6 0.0 copy-start.3
  0.6 0.5 %collective-permute-start.1 = (f32[1,16,16,128]{3,2,1,0:T(8,128)}, f32[1,16,16,128]{3,2,1,0:T(8,128)S(1)}, u32[]{:S(2)}, u32[]{:S(2)}) collective-permute-start(f32[1,16,16,128]{3,2,1,0:T(8,128)} %bitcast.3), channel_id=1, source_target_pairs={{0,8},{8,0},{16,24},{24,16},{1,9},{9,1},{17,25},{25,17},{2,10},{10... | collective-permute-start | bytes 393224 | tf_op jit(solution)/shard_map/ppermute | solution.py:510
  1.2 2.6 %collective-permute-start.3 = (f32[1,16,16,128]{3,2,1,0:T(8,128)}, f32[1,16,16,128]{3,2,1,0:T(8,128)S(1)}, u32[]{:S(2)}, u32[]{:S(2)}) collective-permute-start(f32[1,16,16,128]{3,2,1,0:T(8,128)} %bitcast.4), channel_id=1, source_target_pairs={{0,16},{8,24},{16,0},{24,8},{1,17},{9,25},{17,1},{25,9},{2,18},{10... | collective-permute-start | bytes 393224 | tf_op jit(solution)/shard_map/ppermute | solution.py:510
  3.7 0.0 copy-done.4
  3.7 0.2 collective-permute-start
  3.9 0.0 copy-done.3
  3.9 0.0 copy-start
  3.9 0.9 %copy-done = f32[16,16,128]{2,1,0:T(8,128)S(1)} copy-done((f32[16,16,128]{2,1,0:T(8,128)S(1)}, f32[16,16,128]{2,1,0:T(8,128)}, u32[]{:S(2)}) %copy-start) | copy-done | bytes 131096
  4.8 0.1 first.1
  4.9 0.0 collective-permute-done.refs_1_
  4.9 0.0 collective-permute-done.1.refs_2_.refs_1_
  4.9 0.0 copy-start.1
  5.0 0.1 pack.1
  5.1 0.7 %collective-permute-start.2 = (f32[9,16,128]{2,1,0:T(8,128)S(1)}, f32[9,16,128]{2,1,0:T(8,128)S(1)}, u32[]{:S(2)}, u32[]{:S(2)}) collective-permute-start(f32[9,16,128]{2,1,0:T(8,128)S(1)} %get-tuple-element.27), channel_id=1, source_target_pairs={{1,2},{2,1},{3,4},{4,3},{5,6},{6,5},{8,9},{9,8},{10,11},{11,10},{1... | collective-permute-start | bytes 221192 | tf_op jit(solution)/shard_map/ppermute | solution.py:569
  5.7 2.3 %collective-permute-done.3.refs_1_ = f32[1,16,16,128]{3,2,1,0:T(8,128)S(1)} collective-permute-done((f32[1,16,16,128]{3,2,1,0:T(8,128)}, f32[1,16,16,128]{3,2,1,0:T(8,128)S(1)}, u32[]{:S(2)}, u32[]{:S(2)}) %collective-permute-start.3) | collective-permute-done | bytes 131104 | tf_op jit(solution)/shard_map/ppermute | solution.py:510
  8.0 0.0 collective-permute-done.2.halo
  8.0 2.5 %collective-permute-start.5 = (f32[1,16,16,128]{3,2,1,0:T(8,128)S(1)}, f32[1,16,16,128]{3,2,1,0:T(8,128)S(1)}, u32[]{:S(2)}, u32[]{:S(2)}) collective-permute-start(f32[1,16,16,128]{3,2,1,0:T(8,128)S(1)} %collective-permute-done.3.refs_1_), channel_id=1, source_target_pairs={{0,8},{8,0},{16,24},{24,16},{1,9},{9,1},{17,25},{25,17},{2,10},{10... | collective-permute-start | bytes 393224 | tf_op jit(solution)/shard_map/ppermute | solution.py:510
  10.5 0.0 copy-start.2
  10.5 0.6 %collective-permute-start.4 = (f32[9,16,128]{2,1,0:T(8,128)S(1)}, f32[9,16,128]{2,1,0:T(8,128)S(1)}, u32[]{:S(2)}, u32[]{:S(2)}) collective-permute-start(f32[9,16,128]{2,1,0:T(8,128)S(1)} %join.1), channel_id=1, source_target_pairs={{0,16},{8,24},{16,0},{24,8},{1,17},{9,25},{17,1},{25,9},{2,18},{10... | collective-permute-start | bytes 221192 | tf_op jit(solution)/shard_map/ppermute | solution.py:510
  11.1 0.0 copy-done.1
  11.1 0.3 copy-done.2
  11.4 2.9 %near.1 = (bf16[2,9,128,128]{3,2,1,0:T(8,128)(2,1)S(1)}, bf16[2,9,128,128]{3,2,1,0:T(8,128)(2,1)S(1)}, f32[20,16,256]{2,1,0:T(8,128)S(1)}, f32[12,16,256]{2,1,0:T(8,128)S(1)}, f32[8,128]{1,0:T(8,128)S(1)}) custom-call(f32[9,9,64]{2,1,0:T(8,128)S(1)} %bitcast.7, s32[8,128]{1,0:T(8,128)S(1)} %get-tuple-element.24.radius_ref, ...), custom_call_target="tpu_custom_call" | custom-call | tf_op jit(solution)/shard_map/near/pallas_call | solution.py:520
  14.3 0.7 %collective-permute-done.4.refs_0_ = f32[9,16,128]{2,1,0:T(8,128)S(1)} collective-permute-done((f32[9,16,128]{2,1,0:T(8,128)S(1)}, f32[9,16,128]{2,1,0:T(8,128)S(1)}, u32[]{:S(2)}, u32[]{:S(2)}) %collective-permute-start.4) | collective-permute-done | bytes 73760 | tf_op jit(solution)/shard_map/ppermute | solution.py:510
  14.9 0.0 collective-permute-done.5.refs_2_
  14.9 7.8 %krylov.1 = (f32[32,8,128]{2,1,0:T(8,128)}, f32[3,8,16,128]{3,2,1,0:T(8,128)S(1)}, f32[3,8,16,128]{3,2,1,0:T(8,128)S(1)}, bf16[32,16,256]{2,1,0:T(8,128)(2,1)S(1...) custom-call(f32[9,9,64]{2,1,0:T(8,128)S(1)} %bitcast.8, ...), custom_call_target="tpu_custom_call" | custom-call | tf_op jit(solution)/shard_map/krylov/pallas_call | solution.py:520
  22.8 6.0 %all-to-all-start = ((f32[32,8,128]{2,1,0:T(8,128)}), f32[32,8,128]{2,1,0:T(8,128)S(1)}, u32[]{:S(2)}, u32[]{:S(2)}) async-start(f32[32,8,128]{2,1,0:T(8,128)} %get-tuple-element.35), calls=%async_computation | async-start | bytes 262144 | tf_op jit(solution)/shard_map/all_to_all | solution.py:600
  28.8 0.9 %last.1 = (f32[8,16,128]{2,1,0:T(8,128)S(1)}, f32[8,16,128]{2,1,0:T(8,128)S(1)}) custom-call(f32[8,128]{1,0:T(8,128)S(1)} %get-tuple-element.28.real_ref, bf16[2,9,128,128]{3,2,1,0:T(8,128)(2,1)S(1)} %get-tuple-element.29.nbh, bf16[2,9,128,128]{3,2,1,0:T(8,128)(2,1)S(1)} %get-tuple-element.30.nbl, bf16[2,9,128,128]{3,2,1,0:T(8,128)(2,1)S(1)} %get-tuple-element.37.fbh, ...), custom_call_target="tpu_custom_call" | custom-call | tf_op jit(solution)/shard_map/last/pallas_call | solution.py:520
  29.6 0.3 collective-permute-start.6
  30.0 0.3 collective-permute-start.7
  30.2 1.0 %collective-permute-done.7.other3 = f32[8,16,128]{2,1,0:T(8,128)S(1)} collective-permute-done((f32[8,16,128]{2,1,0:T(8,128)S(1)}, f32[8,16,128]{2,1,0:T(8,128)S(1)}, u32[]{:S(2)}, u32[]{:S(2)}) %collective-permute-start.7) | collective-permute-done | bytes 65568 | tf_op jit(solution)/shard_map/ppermute | solution.py:510
  31.2 0.0 collective-permute-done.6.other_ref
  31.2 5.3 %all-to-all-done.gram_ref = f32[32,8,128]{2,1,0:T(8,128)S(1)} async-done(((f32[32,8,128]{2,1,0:T(8,128)}), f32[32,8,128]{2,1,0:T(8,128)S(1)}, u32[]{:S(2)}, u32[]{:S(2)}) %all-to-all-start) | async-done | bytes 131104 | tf_op jit(solution)/shard_map/all_to_all | solution.py:600
  36.5 2.8 %combine.1 = (f32[16,16,128]{2,1,0:T(8,128)}, f32[16,16,128]{2,1,0:T(8,128)}) custom-call(f32[8,128]{1,0:T(8,128)S(1)} %get-tuple-element.28.real_ref, f32[32,8,128]{2,1,0:T(8,128)S(1)} %all-to-all-done.gram_ref, f32[3,8,16,128]{3,2,1,0:T(8,128)S(1)} %get-tuple-element.36.keep_ref, f32[8,16,128]{2,1,0:T(8,128)S(1)} %get-tuple-element.42.keep3, ...), custom_call_target="tpu_custom_call" | custom-call | tf_op jit(solution)/shard_map/combine/pallas_call | solution.py:520
  (1 shorter events, 0.0 us)
Async XLA Ops:
  0.6 3.1 %copy-start.4 = (s32[1,8]{1,0:T(1,128)S(1)}, s32[1,8]{1,0:T(1,128)}, u32[]{:S(2)}) copy-start(s32[1,8]{1,0:T(1,128)} %refs_0_.1) | copy-start | bytes 100
  0.6 3.3 %copy-start.3 = (s32[64]{0:T(128)S(1)}, s32[64]{0:T(128)}, u32[]{:S(2)}) copy-start(s32[64]{0:T(128)} %param.7) | copy-start | bytes 772
  0.6 4.3 %collective-permute-start.1 = (f32[1,16,16,128]{3,2,1,0:T(8,128)}, f32[1,16,16,128]{3,2,1,0:T(8,128)S(1)}, u32[]{:S(2)}, u32[]{:S(2)}) collective-permute-start(f32[1,16,16,128]{3,2,1,0:T(8,128)} %bitcast.3), channel_id=1, source_target_pairs={{0,8},{8,0},{16,24},{24,16},{1,9},{9,1},{17,25},{25,17},{2,10},{10... | collective-permute-start | bytes 393224 | tf_op jit(solution)/shard_map/ppermute | solution.py:510
  1.2 6.9 %collective-permute-start.3 = (f32[1,16,16,128]{3,2,1,0:T(8,128)}, f32[1,16,16,128]{3,2,1,0:T(8,128)S(1)}, u32[]{:S(2)}, u32[]{:S(2)}) collective-permute-start(f32[1,16,16,128]{3,2,1,0:T(8,128)} %bitcast.4), channel_id=1, source_target_pairs={{0,16},{8,24},{16,0},{24,8},{1,17},{9,25},{17,1},{25,9},{2,18},{10... | collective-permute-start | bytes 393224 | tf_op jit(solution)/shard_map/ppermute | solution.py:510
  3.7 1.2 %collective-permute-start = (s32[1,8]{1,0:T(1,128)S(1)}, s32[1,8]{1,0:T(1,128)S(1)}, u32[]{:S(2)}, u32[]{:S(2)}) collective-permute-start(s32[1,8]{1,0:T(1,128)S(1)} %copy-done.4), channel_id=1, source_target_pairs={{0,8},{8,0},{16,24},{24,16},{1,9},{9,1},{17,25},{25,17},{2,10},{10... | collective-permute-start | bytes 104 | tf_op jit(solution)/shard_map/ppermute | solution.py:510
  3.9 0.9 %copy-start = (f32[16,16,128]{2,1,0:T(8,128)S(1)}, f32[16,16,128]{2,1,0:T(8,128)}, u32[]{:S(2)}) copy-start(f32[16,16,128]{2,1,0:T(8,128)} %param.4) | copy-start | bytes 393220
  4.9 6.1 %copy-start.1 = (f32[16,16,128]{2,1,0:T(8,128)S(1)}, f32[16,16,128]{2,1,0:T(8,128)}, u32[]{:S(2)}) copy-start(f32[16,16,128]{2,1,0:T(8,128)} %param.4) | copy-start | bytes 393220
  5.1 3.0 %collective-permute-start.2 = (f32[9,16,128]{2,1,0:T(8,128)S(1)}, f32[9,16,128]{2,1,0:T(8,128)S(1)}, u32[]{:S(2)}, u32[]{:S(2)}) collective-permute-start(f32[9,16,128]{2,1,0:T(8,128)S(1)} %get-tuple-element.27), channel_id=1, source_target_pairs={{1,2},{2,1},{3,4},{4,3},{5,6},{6,5},{8,9},{9,8},{10,11},{11,10},{1... | collective-permute-start | bytes 221192 | tf_op jit(solution)/shard_map/ppermute | solution.py:569
  8.0 6.9 %collective-permute-start.5 = (f32[1,16,16,128]{3,2,1,0:T(8,128)S(1)}, f32[1,16,16,128]{3,2,1,0:T(8,128)S(1)}, u32[]{:S(2)}, u32[]{:S(2)}) collective-permute-start(f32[1,16,16,128]{3,2,1,0:T(8,128)S(1)} %collective-permute-done.3.refs_1_), channel_id=1, source_target_pairs={{0,8},{8,0},{16,24},{24,16},{1,9},{9,1},{17,25},{25,17},{2,10},{10... | collective-permute-start | bytes 393224 | tf_op jit(solution)/shard_map/ppermute | solution.py:510
  10.5 0.9 %copy-start.2 = (f32[64,9,9]{0,2,1:T(8,128)S(1)}, f32[64,9,9]{0,2,1:T(8,128)}, u32[]{:S(2)}) copy-start(f32[64,9,9]{0,2,1:T(8,128)} %param.6) | copy-start | bytes 62212
  10.5 4.4 %collective-permute-start.4 = (f32[9,16,128]{2,1,0:T(8,128)S(1)}, f32[9,16,128]{2,1,0:T(8,128)S(1)}, u32[]{:S(2)}, u32[]{:S(2)}) collective-permute-start(f32[9,16,128]{2,1,0:T(8,128)S(1)} %join.1), channel_id=1, source_target_pairs={{0,16},{8,24},{16,0},{24,8},{1,17},{9,25},{17,1},{25,9},{2,18},{10... | collective-permute-start | bytes 221192 | tf_op jit(solution)/shard_map/ppermute | solution.py:510
  22.8 13.8 %all-to-all-start = ((f32[32,8,128]{2,1,0:T(8,128)}), f32[32,8,128]{2,1,0:T(8,128)S(1)}, u32[]{:S(2)}, u32[]{:S(2)}) async-start(f32[32,8,128]{2,1,0:T(8,128)} %get-tuple-element.35), calls=%async_computation | async-start | bytes 262144 | tf_op jit(solution)/shard_map/all_to_all | solution.py:600
  29.6 1.6 %collective-permute-start.6 = (f32[3,8,16,128]{3,2,1,0:T(8,128)S(1)}, f32[3,8,16,128]{3,2,1,0:T(8,128)S(1)}, u32[]{:S(2)}, u32[]{:S(2)}) collective-permute-start(f32[3,8,16,128]{3,2,1,0:T(8,128)S(1)} %get-tuple-element.44.send_ref), channel_id=1, source_target_pairs={{0,8},{8,0},{16,24},{24,16},{1,9},{9,1},{17,25},{25,17},{2,10},{10... | collective-permute-start | bytes 589832 | tf_op jit(solution)/shard_map/ppermute | solution.py:510
  30.0 1.3 %collective-permute-start.7 = (f32[8,16,128]{2,1,0:T(8,128)S(1)}, f32[8,16,128]{2,1,0:T(8,128)S(1)}, u32[]{:S(2)}, u32[]{:S(2)}) collective-permute-start(f32[8,16,128]{2,1,0:T(8,128)S(1)} %get-tuple-element.45), channel_id=1, source_target_pairs={{0,8},{8,0},{16,24},{24,16},{1,9},{9,1},{17,25},{25,17},{2,10},{10... | collective-permute-start | bytes 196616 | tf_op jit(solution)/shard_map/ppermute | solution.py:510

commit v3 on v2

--- a/solution.py
+++ b/solution.py
@@ -462,7 +462,7 @@
 
     lines = [line_of(lambda j: at(i + j + 1, j) + damp * at(i + j, j)) for i in range(3)]
     matrix = jnp.concatenate(lines + [line_of(lambda j: at(j, j))], 0)
-    lane = lane_iota(1)
+    lane = lane_iota(64)
     for panel in range(6):
         spread = [
             jnp.broadcast_to(matrix[:, 8 * panel + i : 8 * panel + i + 1], (64, LANES)) for i in range(8)
@@ -471,7 +471,7 @@
             k = 8 * panel + i
             column = spread[i]
             scaled = column * (1.0 / column[k : k + 1, :])
-            matrix = matrix - scaled * (matrix[k : k + 1, :] - (lane == k).astype(F32))
+            matrix = jnp.where(lane == k, scaled, matrix - scaled * matrix[k : k + 1, :])
             for j in range(i + 1, 8):
                 m = 8 * panel + j
                 spread[j] = spread[j] - scaled * column[m : m + 1, :]

time: 39.6 us -> 39.6 us (level)
  no operation moved by 1% of the time
where the time goes in v3:
time: 39.6 us; the launch traced here: 39.3 us
  Pallas kernels  14.6 us (37%)
  starting transfers between devices  13.5 us (34%)
  waiting for transfers between devices  9.26 us (23%)
  local copies, waits for them, and re-layouts  1.24 us (3%)
  between operations  0.73 us (2%)
    pallas_call x7, Pallas kernels, call(): pl.pallas_call(kernel, out_shape=[jax.ShapeDtypeStruct(shape, kind) for s...  14.6 us
    ppermute x7, starting transfers between devices, flip(): return lax.ppermute(value, 'row', [(i, i ^ bit) for i in range(nrow)])  6.85 us
    all_to_all x1, starting transfers between devices, per_device(): grams = lax.all_to_all(grams, ('row', 'col'), 0, 0)  6.01 us
    all_to_all x1, waiting for transfers between devices, per_device(): grams = lax.all_to_all(grams, ('row', 'col'), 0, 0)  5.26 us
    ppermute x7, waiting for transfers between devices, flip(): return lax.ppermute(value, 'row', [(i, i ^ bit) for i in range(nrow)])  3.99 us
    unnamed x10, local copies, waits for them, and re-layouts  1.24 us
  transfers between devices with their start and end apart: 9, of which 4 were waited for; matrix products, arithmetic and copies ran while one was open for 0% of the time, Pallas kernels for 10%

profile of v3, /device:TPU:0, one launch (start us, length us, event | category | flops | bytes accessed | tf_op | source)
XLA Modules:
  0.0 39.3 jit_solution(481315895258220045)
XLA Ops:
  0.6 0.0 copy-start.4
  0.6 0.0 copy-start.3
  0.6 0.5 %collective-permute-start.1 = (f32[1,16,16,128]{3,2,1,0:T(8,128)}, f32[1,16,16,128]{3,2,1,0:T(8,128)S(1)}, u32[]{:S(2)}, u32[]{:S(2)}) collective-permute-start(f32[1,16,16,128]{3,2,1,0:T(8,128)} %bitcast.3), channel_id=1, source_target_pairs={{0,8},{8,0},{16,24},{24,16},{1,9},{9,1},{17,25},{25,17},{2,10},{10... | collective-permute-start | bytes 393224 | tf_op jit(solution)/shard_map/ppermute | solution.py:510
  1.2 2.6 %collective-permute-start.3 = (f32[1,16,16,128]{3,2,1,0:T(8,128)}, f32[1,16,16,128]{3,2,1,0:T(8,128)S(1)}, u32[]{:S(2)}, u32[]{:S(2)}) collective-permute-start(f32[1,16,16,128]{3,2,1,0:T(8,128)} %bitcast.4), channel_id=1, source_target_pairs={{0,16},{8,24},{16,0},{24,8},{1,17},{9,25},{17,1},{25,9},{2,18},{10... | collective-permute-start | bytes 393224 | tf_op jit(solution)/shard_map/ppermute | solution.py:510
  3.7 0.0 copy-done.4
  3.7 0.2 collective-permute-start
  3.9 0.0 copy-done.3
  3.9 0.0 copy-start
  3.9 0.9 %copy-done = f32[16,16,128]{2,1,0:T(8,128)S(1)} copy-done((f32[16,16,128]{2,1,0:T(8,128)S(1)}, f32[16,16,128]{2,1,0:T(8,128)}, u32[]{:S(2)}) %copy-start) | copy-done | bytes 131096
  4.8 0.1 first.1
  4.9 0.0 collective-permute-done.refs_1_
  4.9 0.0 collective-permute-done.1.refs_2_.refs_1_
  4.9 0.0 copy-start.1
  5.0 0.1 pack.1
  5.1 0.7 %collective-permute-start.2 = (f32[9,16,128]{2,1,0:T(8,128)S(1)}, f32[9,16,128]{2,1,0:T(8,128)S(1)}, u32[]{:S(2)}, u32[]{:S(2)}) collective-permute-start(f32[9,16,128]{2,1,0:T(8,128)S(1)} %get-tuple-element.27), channel_id=1, source_target_pairs={{1,2},{2,1},{3,4},{4,3},{5,6},{6,5},{8,9},{9,8},{10,11},{11,10},{1... | collective-permute-start | bytes 221192 | tf_op jit(solution)/shard_map/ppermute | solution.py:569
  5.7 2.3 %collective-permute-done.3.refs_1_ = f32[1,16,16,128]{3,2,1,0:T(8,128)S(1)} collective-permute-done((f32[1,16,16,128]{3,2,1,0:T(8,128)}, f32[1,16,16,128]{3,2,1,0:T(8,128)S(1)}, u32[]{:S(2)}, u32[]{:S(2)}) %collective-permute-start.3) | collective-permute-done | bytes 131104 | tf_op jit(solution)/shard_map/ppermute | solution.py:510
  8.0 0.0 collective-permute-done.2.halo
  8.0 2.5 %collective-permute-start.5 = (f32[1,16,16,128]{3,2,1,0:T(8,128)S(1)}, f32[1,16,16,128]{3,2,1,0:T(8,128)S(1)}, u32[]{:S(2)}, u32[]{:S(2)}) collective-permute-start(f32[1,16,16,128]{3,2,1,0:T(8,128)S(1)} %collective-permute-done.3.refs_1_), channel_id=1, source_target_pairs={{0,8},{8,0},{16,24},{24,16},{1,9},{9,1},{17,25},{25,17},{2,10},{10... | collective-permute-start | bytes 393224 | tf_op jit(solution)/shard_map/ppermute | solution.py:510
  10.5 0.0 copy-start.2
  10.5 0.6 %collective-permute-start.4 = (f32[9,16,128]{2,1,0:T(8,128)S(1)}, f32[9,16,128]{2,1,0:T(8,128)S(1)}, u32[]{:S(2)}, u32[]{:S(2)}) collective-permute-start(f32[9,16,128]{2,1,0:T(8,128)S(1)} %join.1), channel_id=1, source_target_pairs={{0,16},{8,24},{16,0},{24,8},{1,17},{9,25},{17,1},{25,9},{2,18},{10... | collective-permute-start | bytes 221192 | tf_op jit(solution)/shard_map/ppermute | solution.py:510
  11.1 0.0 copy-done.1
  11.1 0.3 copy-done.2
  11.4 2.9 %near.1 = (bf16[2,9,128,128]{3,2,1,0:T(8,128)(2,1)S(1)}, bf16[2,9,128,128]{3,2,1,0:T(8,128)(2,1)S(1)}, f32[20,16,256]{2,1,0:T(8,128)S(1)}, f32[12,16,256]{2,1,0:T(8,128)S(1)}, f32[8,128]{1,0:T(8,128)S(1)}) custom-call(f32[9,9,64]{2,1,0:T(8,128)S(1)} %bitcast.7, s32[8,128]{1,0:T(8,128)S(1)} %get-tuple-element.24.radius_ref, ...), custom_call_target="tpu_custom_call" | custom-call | tf_op jit(solution)/shard_map/near/pallas_call | solution.py:520
  14.3 0.7 %collective-permute-done.4.refs_0_ = f32[9,16,128]{2,1,0:T(8,128)S(1)} collective-permute-done((f32[9,16,128]{2,1,0:T(8,128)S(1)}, f32[9,16,128]{2,1,0:T(8,128)S(1)}, u32[]{:S(2)}, u32[]{:S(2)}) %collective-permute-start.4) | collective-permute-done | bytes 73760 | tf_op jit(solution)/shard_map/ppermute | solution.py:510
  14.9 0.0 collective-permute-done.5.refs_2_
  14.9 7.8 %krylov.1 = (f32[32,8,128]{2,1,0:T(8,128)}, f32[3,8,16,128]{3,2,1,0:T(8,128)S(1)}, f32[3,8,16,128]{3,2,1,0:T(8,128)S(1)}, bf16[32,16,256]{2,1,0:T(8,128)(2,1)S(1...) custom-call(f32[9,9,64]{2,1,0:T(8,128)S(1)} %bitcast.8, ...), custom_call_target="tpu_custom_call" | custom-call | tf_op jit(solution)/shard_map/krylov/pallas_call | solution.py:520
  22.8 6.0 %all-to-all-start = ((f32[32,8,128]{2,1,0:T(8,128)}), f32[32,8,128]{2,1,0:T(8,128)S(1)}, u32[]{:S(2)}, u32[]{:S(2)}) async-start(f32[32,8,128]{2,1,0:T(8,128)} %get-tuple-element.35), calls=%async_computation | async-start | bytes 262144 | tf_op jit(solution)/shard_map/all_to_all | solution.py:600
  28.8 0.9 %last.1 = (f32[8,16,128]{2,1,0:T(8,128)S(1)}, f32[8,16,128]{2,1,0:T(8,128)S(1)}) custom-call(f32[8,128]{1,0:T(8,128)S(1)} %get-tuple-element.28.real_ref, bf16[2,9,128,128]{3,2,1,0:T(8,128)(2,1)S(1)} %get-tuple-element.29.nbh, bf16[2,9,128,128]{3,2,1,0:T(8,128)(2,1)S(1)} %get-tuple-element.30.nbl, bf16[2,9,128,128]{3,2,1,0:T(8,128)(2,1)S(1)} %get-tuple-element.37.fbh, ...), custom_call_target="tpu_custom_call" | custom-call | tf_op jit(solution)/shard_map/last/pallas_call | solution.py:520
  29.6 0.3 collective-permute-start.6
  30.0 0.3 collective-permute-start.7
  30.2 1.0 %collective-permute-done.7.other3 = f32[8,16,128]{2,1,0:T(8,128)S(1)} collective-permute-done((f32[8,16,128]{2,1,0:T(8,128)S(1)}, f32[8,16,128]{2,1,0:T(8,128)S(1)}, u32[]{:S(2)}, u32[]{:S(2)}) %collective-permute-start.7) | collective-permute-done | bytes 65568 | tf_op jit(solution)/shard_map/ppermute | solution.py:510
  31.2 0.0 collective-permute-done.6.other_ref
  31.2 5.3 %all-to-all-done.gram_ref = f32[32,8,128]{2,1,0:T(8,128)S(1)} async-done(((f32[32,8,128]{2,1,0:T(8,128)}), f32[32,8,128]{2,1,0:T(8,128)S(1)}, u32[]{:S(2)}, u32[]{:S(2)}) %all-to-all-start) | async-done | bytes 131104 | tf_op jit(solution)/shard_map/all_to_all | solution.py:600
  36.5 2.8 %combine.1 = (f32[16,16,128]{2,1,0:T(8,128)}, f32[16,16,128]{2,1,0:T(8,128)}) custom-call(f32[8,128]{1,0:T(8,128)S(1)} %get-tuple-element.28.real_ref, f32[32,8,128]{2,1,0:T(8,128)S(1)} %all-to-all-done.gram_ref, f32[3,8,16,128]{3,2,1,0:T(8,128)S(1)} %get-tuple-element.36.keep_ref, f32[8,16,128]{2,1,0:T(8,128)S(1)} %get-tuple-element.42.keep3, ...), custom_call_target="tpu_custom_call" | custom-call | tf_op jit(solution)/shard_map/combine/pallas_call | solution.py:520
  (1 shorter events, 0.0 us)
Async XLA Ops:
  0.6 3.1 %copy-start.4 = (s32[1,8]{1,0:T(1,128)S(1)}, s32[1,8]{1,0:T(1,128)}, u32[]{:S(2)}) copy-start(s32[1,8]{1,0:T(1,128)} %refs_0_.1) | copy-start | bytes 100
  0.6 3.3 %copy-start.3 = (s32[64]{0:T(128)S(1)}, s32[64]{0:T(128)}, u32[]{:S(2)}) copy-start(s32[64]{0:T(128)} %param.7) | copy-start | bytes 772
  0.6 4.3 %collective-permute-start.1 = (f32[1,16,16,128]{3,2,1,0:T(8,128)}, f32[1,16,16,128]{3,2,1,0:T(8,128)S(1)}, u32[]{:S(2)}, u32[]{:S(2)}) collective-permute-start(f32[1,16,16,128]{3,2,1,0:T(8,128)} %bitcast.3), channel_id=1, source_target_pairs={{0,8},{8,0},{16,24},{24,16},{1,9},{9,1},{17,25},{25,17},{2,10},{10... | collective-permute-start | bytes 393224 | tf_op jit(solution)/shard_map/ppermute | solution.py:510
  1.2 6.9 %collective-permute-start.3 = (f32[1,16,16,128]{3,2,1,0:T(8,128)}, f32[1,16,16,128]{3,2,1,0:T(8,128)S(1)}, u32[]{:S(2)}, u32[]{:S(2)}) collective-permute-start(f32[1,16,16,128]{3,2,1,0:T(8,128)} %bitcast.4), channel_id=1, source_target_pairs={{0,16},{8,24},{16,0},{24,8},{1,17},{9,25},{17,1},{25,9},{2,18},{10... | collective-permute-start | bytes 393224 | tf_op jit(solution)/shard_map/ppermute | solution.py:510
  3.7 1.2 %collective-permute-start = (s32[1,8]{1,0:T(1,128)S(1)}, s32[1,8]{1,0:T(1,128)S(1)}, u32[]{:S(2)}, u32[]{:S(2)}) collective-permute-start(s32[1,8]{1,0:T(1,128)S(1)} %copy-done.4), channel_id=1, source_target_pairs={{0,8},{8,0},{16,24},{24,16},{1,9},{9,1},{17,25},{25,17},{2,10},{10... | collective-permute-start | bytes 104 | tf_op jit(solution)/shard_map/ppermute | solution.py:510
  3.9 0.9 %copy-start = (f32[16,16,128]{2,1,0:T(8,128)S(1)}, f32[16,16,128]{2,1,0:T(8,128)}, u32[]{:S(2)}) copy-start(f32[16,16,128]{2,1,0:T(8,128)} %param.4) | copy-start | bytes 393220
  4.9 6.1 %copy-start.1 = (f32[16,16,128]{2,1,0:T(8,128)S(1)}, f32[16,16,128]{2,1,0:T(8,128)}, u32[]{:S(2)}) copy-start(f32[16,16,128]{2,1,0:T(8,128)} %param.4) | copy-start | bytes 393220
  5.1 3.0 %collective-permute-start.2 = (f32[9,16,128]{2,1,0:T(8,128)S(1)}, f32[9,16,128]{2,1,0:T(8,128)S(1)}, u32[]{:S(2)}, u32[]{:S(2)}) collective-permute-start(f32[9,16,128]{2,1,0:T(8,128)S(1)} %get-tuple-element.27), channel_id=1, source_target_pairs={{1,2},{2,1},{3,4},{4,3},{5,6},{6,5},{8,9},{9,8},{10,11},{11,10},{1... | collective-permute-start | bytes 221192 | tf_op jit(solution)/shard_map/ppermute | solution.py:569
  8.0 6.9 %collective-permute-start.5 = (f32[1,16,16,128]{3,2,1,0:T(8,128)S(1)}, f32[1,16,16,128]{3,2,1,0:T(8,128)S(1)}, u32[]{:S(2)}, u32[]{:S(2)}) collective-permute-start(f32[1,16,16,128]{3,2,1,0:T(8,128)S(1)} %collective-permute-done.3.refs_1_), channel_id=1, source_target_pairs={{0,8},{8,0},{16,24},{24,16},{1,9},{9,1},{17,25},{25,17},{2,10},{10... | collective-permute-start | bytes 393224 | tf_op jit(solution)/shard_map/ppermute | solution.py:510
  10.5 0.9 %copy-start.2 = (f32[64,9,9]{0,2,1:T(8,128)S(1)}, f32[64,9,9]{0,2,1:T(8,128)}, u32[]{:S(2)}) copy-start(f32[64,9,9]{0,2,1:T(8,128)} %param.6) | copy-start | bytes 62212
  10.5 4.4 %collective-permute-start.4 = (f32[9,16,128]{2,1,0:T(8,128)S(1)}, f32[9,16,128]{2,1,0:T(8,128)S(1)}, u32[]{:S(2)}, u32[]{:S(2)}) collective-permute-start(f32[9,16,128]{2,1,0:T(8,128)S(1)} %join.1), channel_id=1, source_target_pairs={{0,16},{8,24},{16,0},{24,8},{1,17},{9,25},{17,1},{25,9},{2,18},{10... | collective-permute-start | bytes 221192 | tf_op jit(solution)/shard_map/ppermute | solution.py:510
  22.8 13.8 %all-to-all-start = ((f32[32,8,128]{2,1,0:T(8,128)}), f32[32,8,128]{2,1,0:T(8,128)S(1)}, u32[]{:S(2)}, u32[]{:S(2)}) async-start(f32[32,8,128]{2,1,0:T(8,128)} %get-tuple-element.35), calls=%async_computation | async-start | bytes 262144 | tf_op jit(solution)/shard_map/all_to_all | solution.py:600
  29.6 1.6 %collective-permute-start.6 = (f32[3,8,16,128]{3,2,1,0:T(8,128)S(1)}, f32[3,8,16,128]{3,2,1,0:T(8,128)S(1)}, u32[]{:S(2)}, u32[]{:S(2)}) collective-permute-start(f32[3,8,16,128]{3,2,1,0:T(8,128)S(1)} %get-tuple-element.44.send_ref), channel_id=1, source_target_pairs={{0,8},{8,0},{16,24},{24,16},{1,9},{9,1},{17,25},{25,17},{2,10},{10... | collective-permute-start | bytes 589832 | tf_op jit(solution)/shard_map/ppermute | solution.py:510
  30.0 1.3 %collective-permute-start.7 = (f32[8,16,128]{2,1,0:T(8,128)S(1)}, f32[8,16,128]{2,1,0:T(8,128)S(1)}, u32[]{:S(2)}, u32[]{:S(2)}) collective-permute-start(f32[8,16,128]{2,1,0:T(8,128)S(1)} %get-tuple-element.45), channel_id=1, source_target_pairs={{0,8},{8,0},{16,24},{24,16},{1,9},{9,1},{17,25},{25,17},{2,10},{10... | collective-permute-start | bytes 196616 | tf_op jit(solution)/shard_map/ppermute | solution.py:510

commit v4 on v3

--- a/solution.py
+++ b/solution.py
@@ -367,25 +367,23 @@
             acc[...] = jnp.zeros_like(acc)
         where.each(lambda s: spread_rows(bands, uh, ul, 0, acc, s), into, first)
         finish(n, out)
+    for ref, row in zip((keep_ref, send_ref), where.own()):
+        for n in range(NB - 1):
+            for p in range(8):
+                ref[n, p] = halves(kr[n, row * 8 + p])
+    gram, blank = jnp.zeros((NB * 16, NB * 16), F32), jnp.zeros((16, 2 * LANES), F32)
+    for p in range(8):
+        stack = [jnp.concatenate([ref[n, p] for n in range(NB - 1)], 0) for ref in (keep_ref, send_ref)]
+        gram = gram + exact_gram(jnp.concatenate([jnp.concatenate(stack, 1), blank], 0))
+    gram = jnp.concatenate([gram, jnp.zeros_like(gram)], 1)
     forward(0, fewer, True)
-
-    for side, (ref, row) in enumerate(zip((keep_ref, send_ref), where.own())):
-        for n in range(NB):
-            for p in range(8):
-                value = halves(kr[n, row * 8 + p])
-                if n < NB - 1:
-                    ref[n, p] = value
-                else:
-                    extra[side, p] = value
-    gram = jnp.zeros((NB * 16, NB * 16), F32)
+    final = jnp.zeros((16, 16), F32)
+    mine, pair = where.own()
     for p in range(8):
-        stack = [
-            jnp.concatenate([ref[n, p] for n in range(NB - 1)] + [extra[side, p]], 0)
-            for side, ref in enumerate((keep_ref, send_ref))
-        ]
-        stack = jnp.concatenate(stack, 1)
-        gram = gram + exact_gram(stack)
-    gram = jnp.concatenate([gram, jnp.zeros_like(gram)], 1)
+        stack = [halves(kr[NB - 1, row * 8 + p]) for row in (mine, pair)]
+        final = final + exact_gram(jnp.concatenate(stack, 1))
+    extra[...] = jnp.zeros_like(extra)
+    extra[:, :16] = final
     lanes, sub = lane_iota(16), lax.broadcasted_iota(jnp.int32, (16, LANES), 0)
     rel = lanes & 15
 
@@ -395,7 +393,7 @@
     message = jnp.zeros((16, LANES), F32)
     for a in range(NB - 1):
         even = moved(a, a, a)
-        odd = moved(a, a + 1, a) if a < NB - 2 else moved(a + 1, a + 1, a) - shift[:, :LANES] * even
+        odd = moved(a, a + 1, a) if a < NB - 2 else pltpu.roll(extra[...], 16 * a, 1) - shift[:, :LANES] * even
         here = lanes >> 4 == a
         message = jnp.where(here, jnp.where(sub >= rel, even, odd), message)
         corner = jnp.sum(jnp.where(here & (sub == rel), odd, 0.0), axis=1, keepdims=True)
@@ -592,7 +590,7 @@
         [taps, reach, real, nbh, nbl, nacc, nacc1, *far],
         [bases_of(extra)]
         + [rows_of(pairs + 4, BF16)] * 2
-        + [rows_of(pairs + 4, F32), ((NB, pairs, 16, 2 * LANES), F32), ((2, 8, 16, LANES), F32)]
+        + [rows_of(pairs + 4, F32), ((NB, pairs, 16, 2 * LANES), F32), ((16, LANES), F32)]
         + [((share, 8, LANES), F32), pltpu.SemaphoreType.DMA((ndev // share,))],
         8 + 3 * nrow,
         [pl.BlockSpec(memory_space=pl.ANY)] + [VMEM] * (len(out) - 1),

time: 39.6 us -> 40.5 us (1.023)
  Pallas kernels: 14.6 us -> 15.5 us
    pallas_call x7, Pallas kernels: 14.6 us -> 15.5 us  [call(): pl.pallas_call(kernel, out_shape=[jax.ShapeDtypeStruct(shape, kind) for s...]
where the time goes in v4:
time: 40.5 us; the launch traced here: 40.3 us
  Pallas kernels  15.5 us (38%)
  starting transfers between devices  13.5 us (33%)
  waiting for transfers between devices  9.26 us (23%)
  local copies, waits for them, and re-layouts  1.24 us (3%)
  between operations  0.73 us (2%)
    pallas_call x7, Pallas kernels, call(): pl.pallas_call(kernel, out_shape=[jax.ShapeDtypeStruct(shape, kind) for s...  15.5 us
    ppermute x7, starting transfers between devices, flip(): return lax.ppermute(value, 'row', [(i, i ^ bit) for i in range(nrow)])  6.85 us
    all_to_all x1, starting transfers between devices, per_device(): grams = lax.all_to_all(grams, ('row', 'col'), 0, 0)  6.03 us
    all_to_all x1, waiting for transfers between devices, per_device(): grams = lax.all_to_all(grams, ('row', 'col'), 0, 0)  5.27 us
    ppermute x7, waiting for transfers between devices, flip(): return lax.ppermute(value, 'row', [(i, i ^ bit) for i in range(nrow)])  3.99 us
    unnamed x10, local copies, waits for them, and re-layouts  1.24 us
  transfers between devices with their start and end apart: 9, of which 4 were waited for; matrix products, arithmetic and copies ran while one was open for 0% of the time, Pallas kernels for 10%

profile of v4, /device:TPU:0, one launch (start us, length us, event | category | flops | bytes accessed | tf_op | source)
XLA Modules:
  0.0 40.3 jit_solution(4523716606381022987)
XLA Ops:
  0.6 0.0 copy-start.4
  0.6 0.0 copy-start.3
  0.6 0.5 %collective-permute-start.1 = (f32[1,16,16,128]{3,2,1,0:T(8,128)}, f32[1,16,16,128]{3,2,1,0:T(8,128)S(1)}, u32[]{:S(2)}, u32[]{:S(2)}) collective-permute-start(f32[1,16,16,128]{3,2,1,0:T(8,128)} %bitcast.3), channel_id=1, source_target_pairs={{0,8},{8,0},{16,24},{24,16},{1,9},{9,1},{17,25},{25,17},{2,10},{10... | collective-permute-start | bytes 393224 | tf_op jit(solution)/shard_map/ppermute | solution.py:508
  1.2 2.6 %collective-permute-start.3 = (f32[1,16,16,128]{3,2,1,0:T(8,128)}, f32[1,16,16,128]{3,2,1,0:T(8,128)S(1)}, u32[]{:S(2)}, u32[]{:S(2)}) collective-permute-start(f32[1,16,16,128]{3,2,1,0:T(8,128)} %bitcast.4), channel_id=1, source_target_pairs={{0,16},{8,24},{16,0},{24,8},{1,17},{9,25},{17,1},{25,9},{2,18},{10... | collective-permute-start | bytes 393224 | tf_op jit(solution)/shard_map/ppermute | solution.py:508
  3.7 0.0 copy-done.4
  3.7 0.2 collective-permute-start
  3.9 0.0 copy-done.3
  3.9 0.0 copy-start
  3.9 0.9 %copy-done = f32[16,16,128]{2,1,0:T(8,128)S(1)} copy-done((f32[16,16,128]{2,1,0:T(8,128)S(1)}, f32[16,16,128]{2,1,0:T(8,128)}, u32[]{:S(2)}) %copy-start) | copy-done | bytes 131096
  4.8 0.1 first.1
  4.9 0.0 collective-permute-done.refs_1_
  4.9 0.0 collective-permute-done.1.refs_2_.refs_1_
  4.9 0.0 copy-start.1
  5.0 0.1 pack.1
  5.1 0.7 %collective-permute-start.2 = (f32[9,16,128]{2,1,0:T(8,128)S(1)}, f32[9,16,128]{2,1,0:T(8,128)S(1)}, u32[]{:S(2)}, u32[]{:S(2)}) collective-permute-start(f32[9,16,128]{2,1,0:T(8,128)S(1)} %get-tuple-element.27), channel_id=1, source_target_pairs={{1,2},{2,1},{3,4},{4,3},{5,6},{6,5},{8,9},{9,8},{10,11},{11,10},{1... | collective-permute-start | bytes 221192 | tf_op jit(solution)/shard_map/ppermute | solution.py:567
  5.7 2.3 %collective-permute-done.3.refs_1_ = f32[1,16,16,128]{3,2,1,0:T(8,128)S(1)} collective-permute-done((f32[1,16,16,128]{3,2,1,0:T(8,128)}, f32[1,16,16,128]{3,2,1,0:T(8,128)S(1)}, u32[]{:S(2)}, u32[]{:S(2)}) %collective-permute-start.3) | collective-permute-done | bytes 131104 | tf_op jit(solution)/shard_map/ppermute | solution.py:508
  8.0 0.0 collective-permute-done.2.halo
  8.0 2.5 %collective-permute-start.5 = (f32[1,16,16,128]{3,2,1,0:T(8,128)S(1)}, f32[1,16,16,128]{3,2,1,0:T(8,128)S(1)}, u32[]{:S(2)}, u32[]{:S(2)}) collective-permute-start(f32[1,16,16,128]{3,2,1,0:T(8,128)S(1)} %collective-permute-done.3.refs_1_), channel_id=1, source_target_pairs={{0,8},{8,0},{16,24},{24,16},{1,9},{9,1},{17,25},{25,17},{2,10},{10... | collective-permute-start | bytes 393224 | tf_op jit(solution)/shard_map/ppermute | solution.py:508
  10.5 0.0 copy-start.2
  10.5 0.6 %collective-permute-start.4 = (f32[9,16,128]{2,1,0:T(8,128)S(1)}, f32[9,16,128]{2,1,0:T(8,128)S(1)}, u32[]{:S(2)}, u32[]{:S(2)}) collective-permute-start(f32[9,16,128]{2,1,0:T(8,128)S(1)} %join.1), channel_id=1, source_target_pairs={{0,16},{8,24},{16,0},{24,8},{1,17},{9,25},{17,1},{25,9},{2,18},{10... | collective-permute-start | bytes 221192 | tf_op jit(solution)/shard_map/ppermute | solution.py:508
  11.1 0.0 copy-done.1
  11.1 0.3 copy-done.2
  11.4 2.9 %near.1 = (bf16[2,9,128,128]{3,2,1,0:T(8,128)(2,1)S(1)}, bf16[2,9,128,128]{3,2,1,0:T(8,128)(2,1)S(1)}, f32[20,16,256]{2,1,0:T(8,128)S(1)}, f32[12,16,256]{2,1,0:T(8,128)S(1)}, f32[8,128]{1,0:T(8,128)S(1)}) custom-call(f32[9,9,64]{2,1,0:T(8,128)S(1)} %bitcast.7, s32[8,128]{1,0:T(8,128)S(1)} %get-tuple-element.24.radius_ref, ...), custom_call_target="tpu_custom_call" | custom-call | tf_op jit(solution)/shard_map/near/pallas_call | solution.py:518
  14.3 0.7 %collective-permute-done.4.refs_0_ = f32[9,16,128]{2,1,0:T(8,128)S(1)} collective-permute-done((f32[9,16,128]{2,1,0:T(8,128)S(1)}, f32[9,16,128]{2,1,0:T(8,128)S(1)}, u32[]{:S(2)}, u32[]{:S(2)}) %collective-permute-start.4) | collective-permute-done | bytes 73760 | tf_op jit(solution)/shard_map/ppermute | solution.py:508
  14.9 0.0 collective-permute-done.5.refs_2_
  14.9 8.7 %krylov.1 = (f32[32,8,128]{2,1,0:T(8,128)}, f32[3,8,16,128]{3,2,1,0:T(8,128)S(1)}, f32[3,8,16,128]{3,2,1,0:T(8,128)S(1)}, bf16[32,16,256]{2,1,0:T(8,128)(2,1)S(1...) custom-call(f32[9,9,64]{2,1,0:T(8,128)S(1)} %bitcast.8, ...), custom_call_target="tpu_custom_call" | custom-call | tf_op jit(solution)/shard_map/krylov/pallas_call | solution.py:518
  23.7 6.0 %all-to-all-start = ((f32[32,8,128]{2,1,0:T(8,128)}), f32[32,8,128]{2,1,0:T(8,128)S(1)}, u32[]{:S(2)}, u32[]{:S(2)}) async-start(f32[32,8,128]{2,1,0:T(8,128)} %get-tuple-element.35), calls=%async_computation | async-start | bytes 262144 | tf_op jit(solution)/shard_map/all_to_all | solution.py:598
  29.7 0.9 %last.1 = (f32[8,16,128]{2,1,0:T(8,128)S(1)}, f32[8,16,128]{2,1,0:T(8,128)S(1)}) custom-call(f32[8,128]{1,0:T(8,128)S(1)} %get-tuple-element.28.real_ref, bf16[2,9,128,128]{3,2,1,0:T(8,128)(2,1)S(1)} %get-tuple-element.29.nbh, bf16[2,9,128,128]{3,2,1,0:T(8,128)(2,1)S(1)} %get-tuple-element.30.nbl, bf16[2,9,128,128]{3,2,1,0:T(8,128)(2,1)S(1)} %get-tuple-element.37.fbh, ...), custom_call_target="tpu_custom_call" | custom-call | tf_op jit(solution)/shard_map/last/pallas_call | solution.py:518
  30.6 0.3 collective-permute-start.6
  30.9 0.3 collective-permute-start.7
  31.2 1.0 %collective-permute-done.7.other3 = f32[8,16,128]{2,1,0:T(8,128)S(1)} collective-permute-done((f32[8,16,128]{2,1,0:T(8,128)S(1)}, f32[8,16,128]{2,1,0:T(8,128)S(1)}, u32[]{:S(2)}, u32[]{:S(2)}) %collective-permute-start.7) | collective-permute-done | bytes 65568 | tf_op jit(solution)/shard_map/ppermute | solution.py:508
  32.2 0.0 collective-permute-done.6.other_ref
  32.2 5.3 %all-to-all-done.gram_ref = f32[32,8,128]{2,1,0:T(8,128)S(1)} async-done(((f32[32,8,128]{2,1,0:T(8,128)}), f32[32,8,128]{2,1,0:T(8,128)S(1)}, u32[]{:S(2)}, u32[]{:S(2)}) %all-to-all-start) | async-done | bytes 131104 | tf_op jit(solution)/shard_map/all_to_all | solution.py:598
  37.5 2.8 %combine.1 = (f32[16,16,128]{2,1,0:T(8,128)}, f32[16,16,128]{2,1,0:T(8,128)}) custom-call(f32[8,128]{1,0:T(8,128)S(1)} %get-tuple-element.28.real_ref, f32[32,8,128]{2,1,0:T(8,128)S(1)} %all-to-all-done.gram_ref, f32[3,8,16,128]{3,2,1,0:T(8,128)S(1)} %get-tuple-element.36.keep_ref, f32[8,16,128]{2,1,0:T(8,128)S(1)} %get-tuple-element.42.keep3, ...), custom_call_target="tpu_custom_call" | custom-call | tf_op jit(solution)/shard_map/combine/pallas_call | solution.py:518
  (1 shorter events, 0.0 us)
Async XLA Ops:
  0.6 3.1 %copy-start.4 = (s32[1,8]{1,0:T(1,128)S(1)}, s32[1,8]{1,0:T(1,128)}, u32[]{:S(2)}) copy-start(s32[1,8]{1,0:T(1,128)} %refs_0_.1) | copy-start | bytes 100
  0.6 3.3 %copy-start.3 = (s32[64]{0:T(128)S(1)}, s32[64]{0:T(128)}, u32[]{:S(2)}) copy-start(s32[64]{0:T(128)} %param.7) | copy-start | bytes 772
  0.6 4.3 %collective-permute-start.1 = (f32[1,16,16,128]{3,2,1,0:T(8,128)}, f32[1,16,16,128]{3,2,1,0:T(8,128)S(1)}, u32[]{:S(2)}, u32[]{:S(2)}) collective-permute-start(f32[1,16,16,128]{3,2,1,0:T(8,128)} %bitcast.3), channel_id=1, source_target_pairs={{0,8},{8,0},{16,24},{24,16},{1,9},{9,1},{17,25},{25,17},{2,10},{10... | collective-permute-start | bytes 393224 | tf_op jit(solution)/shard_map/ppermute | solution.py:508
  1.2 6.9 %collective-permute-start.3 = (f32[1,16,16,128]{3,2,1,0:T(8,128)}, f32[1,16,16,128]{3,2,1,0:T(8,128)S(1)}, u32[]{:S(2)}, u32[]{:S(2)}) collective-permute-start(f32[1,16,16,128]{3,2,1,0:T(8,128)} %bitcast.4), channel_id=1, source_target_pairs={{0,16},{8,24},{16,0},{24,8},{1,17},{9,25},{17,1},{25,9},{2,18},{10... | collective-permute-start | bytes 393224 | tf_op jit(solution)/shard_map/ppermute | solution.py:508
  3.7 1.2 %collective-permute-start = (s32[1,8]{1,0:T(1,128)S(1)}, s32[1,8]{1,0:T(1,128)S(1)}, u32[]{:S(2)}, u32[]{:S(2)}) collective-permute-start(s32[1,8]{1,0:T(1,128)S(1)} %copy-done.4), channel_id=1, source_target_pairs={{0,8},{8,0},{16,24},{24,16},{1,9},{9,1},{17,25},{25,17},{2,10},{10... | collective-permute-start | bytes 104 | tf_op jit(solution)/shard_map/ppermute | solution.py:508
  3.9 0.9 %copy-start = (f32[16,16,128]{2,1,0:T(8,128)S(1)}, f32[16,16,128]{2,1,0:T(8,128)}, u32[]{:S(2)}) copy-start(f32[16,16,128]{2,1,0:T(8,128)} %param.4) | copy-start | bytes 393220
  4.9 6.1 %copy-start.1 = (f32[16,16,128]{2,1,0:T(8,128)S(1)}, f32[16,16,128]{2,1,0:T(8,128)}, u32[]{:S(2)}) copy-start(f32[16,16,128]{2,1,0:T(8,128)} %param.4) | copy-start | bytes 393220
  5.1 3.0 %collective-permute-start.2 = (f32[9,16,128]{2,1,0:T(8,128)S(1)}, f32[9,16,128]{2,1,0:T(8,128)S(1)}, u32[]{:S(2)}, u32[]{:S(2)}) collective-permute-start(f32[9,16,128]{2,1,0:T(8,128)S(1)} %get-tuple-element.27), channel_id=1, source_target_pairs={{1,2},{2,1},{3,4},{4,3},{5,6},{6,5},{8,9},{9,8},{10,11},{11,10},{1... | collective-permute-start | bytes 221192 | tf_op jit(solution)/shard_map/ppermute | solution.py:567
  8.0 6.9 %collective-permute-start.5 = (f32[1,16,16,128]{3,2,1,0:T(8,128)S(1)}, f32[1,16,16,128]{3,2,1,0:T(8,128)S(1)}, u32[]{:S(2)}, u32[]{:S(2)}) collective-permute-start(f32[1,16,16,128]{3,2,1,0:T(8,128)S(1)} %collective-permute-done.3.refs_1_), channel_id=1, source_target_pairs={{0,8},{8,0},{16,24},{24,16},{1,9},{9,1},{17,25},{25,17},{2,10},{10... | collective-permute-start | bytes 393224 | tf_op jit(solution)/shard_map/ppermute | solution.py:508
  10.5 0.9 %copy-start.2 = (f32[64,9,9]{0,2,1:T(8,128)S(1)}, f32[64,9,9]{0,2,1:T(8,128)}, u32[]{:S(2)}) copy-start(f32[64,9,9]{0,2,1:T(8,128)} %param.6) | copy-start | bytes 62212
  10.5 4.4 %collective-permute-start.4 = (f32[9,16,128]{2,1,0:T(8,128)S(1)}, f32[9,16,128]{2,1,0:T(8,128)S(1)}, u32[]{:S(2)}, u32[]{:S(2)}) collective-permute-start(f32[9,16,128]{2,1,0:T(8,128)S(1)} %join.1), channel_id=1, source_target_pairs={{0,16},{8,24},{16,0},{24,8},{1,17},{9,25},{17,1},{25,9},{2,18},{10... | collective-permute-start | bytes 221192 | tf_op jit(solution)/shard_map/ppermute | solution.py:508
  23.7 13.8 %all-to-all-start = ((f32[32,8,128]{2,1,0:T(8,128)}), f32[32,8,128]{2,1,0:T(8,128)S(1)}, u32[]{:S(2)}, u32[]{:S(2)}) async-start(f32[32,8,128]{2,1,0:T(8,128)} %get-tuple-element.35), calls=%async_computation | async-start | bytes 262144 | tf_op jit(solution)/shard_map/all_to_all | solution.py:598
  30.6 1.6 %collective-permute-start.6 = (f32[3,8,16,128]{3,2,1,0:T(8,128)S(1)}, f32[3,8,16,128]{3,2,1,0:T(8,128)S(1)}, u32[]{:S(2)}, u32[]{:S(2)}) collective-permute-start(f32[3,8,16,128]{3,2,1,0:T(8,128)S(1)} %get-tuple-element.44.send_ref), channel_id=1, source_target_pairs={{0,8},{8,0},{16,24},{24,16},{1,9},{9,1},{17,25},{25,17},{2,10},{10... | collective-permute-start | bytes 589832 | tf_op jit(solution)/shard_map/ppermute | solution.py:508
  30.9 1.3 %collective-permute-start.7 = (f32[8,16,128]{2,1,0:T(8,128)S(1)}, f32[8,16,128]{2,1,0:T(8,128)S(1)}, u32[]{:S(2)}, u32[]{:S(2)}) collective-permute-start(f32[8,16,128]{2,1,0:T(8,128)S(1)} %get-tuple-element.45), channel_id=1, source_target_pairs={{0,8},{8,0},{16,24},{24,16},{1,9},{9,1},{17,25},{25,17},{2,10},{10... | collective-permute-start | bytes 196616 | tf_op jit(solution)/shard_map/ppermute | solution.py:508
